TPU v7x, 256 devices: a whole 4x4x8 slice. The times are simulated.
256 devices in a mesh: dp: 32 (over y, x, core), vocab: 8 (over z).
Axes of the slice: x: 4, y: 4, z: 8, core: 2. Of those that a mesh axis runs over, the one named last changes fastest.
Arguments:
- embedding: bfloat16 [4096, 4608], P('vocab'), may hold values from -0.36 to 0.36
- hidden: bfloat16 [16384, 4608], P('dp'), may hold values from -2 to 2
- targets: int32 [16384], P('dp'), may hold values from 0 to 4095
- input_ids: int32 [16384], P('dp'), may hold values from 0 to 4095, as said below
- input_grad: bfloat16 [16384, 4608], P('dp', 'vocab'), may hold values from -6 to 6
Outputs:
- token_loss: float32 [16384], P('dp')
- hidden_grad: float32 [16384, 4608], P('dp', 'vocab')
- embed_grad: float32 [4096, 4608], P('vocab', 'dp')
Inputs may be any that keep to these rules, and one draw needn't show every extreme that they name: `input_ids`: within each data group's 512 tokens (aligned blocks), at most 256 ids lie in any one vocabulary shard of 512 rows, and some shard holds exactly 256 of them in every group.
All inputs are finite; a program needn't handle non-finite values.
Results may differ from a plain program's by a relative error of at most 0.0018.
Values may be sent and summed in bfloat16 or wider, within the bound.
No kernel may reach another device: no remote copies, remote signals or barrier semaphores. Data moves between devices by JAX's collectives and lax.ppermute only.
A program may use at most 128 MiB of HBM per device.

v0:
```python
import jax
import jax.numpy as jnp
from jax import lax
from jax.sharding import PartitionSpec as P

softcap = 30.0


def per_device(embedding, hidden, targets, input_ids, input_grad):
    vocab_rows = embedding.shape[0]
    my_shard = lax.axis_index("vocab")
    offset = my_shard * vocab_rows
    logits = jnp.einsum("td,vd->tv", hidden, embedding, preferred_element_type=jnp.float32)
    capped = softcap * jnp.tanh(logits / softcap)
    exponent = jnp.exp(capped)
    row_index = jnp.arange(vocab_rows, dtype=jnp.int32)
    target_hit = (row_index[None, :] == (targets - offset)[:, None]).astype(jnp.float32)
    denominator, picked = lax.psum(
        (jnp.sum(exponent, axis=1), jnp.sum(target_hit * capped, axis=1)), "vocab"
    )
    token_loss = jnp.log(denominator) - picked
    scaled = (
        (exponent / denominator[:, None] - target_hit) * (1.0 - (capped / softcap) ** 2)
    ).astype(jnp.bfloat16)
    partial_grad = jnp.einsum("tv,vd->td", scaled, embedding, preferred_element_type=jnp.float32)
    hidden_grad = lax.psum_scatter(partial_grad, "vocab", scatter_dimension=1, tiled=True)
    tied_part = jnp.einsum("tv,td->vd", scaled, hidden, preferred_element_type=jnp.float32)
    owner_hit = (row_index[:, None] == (input_ids - offset)[None, :]).astype(jnp.bfloat16)
    input_part = jnp.dot(
        owner_hit,
        lax.all_gather(input_grad, "vocab", axis=1, tiled=True),
        preferred_element_type=jnp.float32,
    )
    embed_grad = lax.psum_scatter(tied_part + input_part, "dp", scatter_dimension=1, tiled=True)
    return (token_loss, hidden_grad, embed_grad)


def solution(mesh):
    return jax.shard_map(
        per_device,
        mesh=mesh,
        in_specs=(P("vocab", None), P("dp", None), P("dp"), P("dp"), P("dp", "vocab")),
        out_specs=(P("dp"), P("dp", "vocab"), P("vocab", "dp")),
        check_vma=False,
    )
```

profile of v0, /device:TPU:2, one launch (start us, length us, event | category | flops | bytes accessed | tf_op | source)
XLA Modules:
  0.0 291.9 jit_solution(8984423568192248924)
XLA Ops:
  7.2 0.0 all-gather.2.cloned.1.call-start
  7.2 0.7 all-gather.2.cloned.1.call-update
  7.9 0.0 reduce-scatter.3.cloned.1.call-start
  7.9 0.7 broadcast_subtract_fusion.1
  8.6 6.1 %exponential_reduce_fusion = (f32[512]{0:T(512)S(1)}, f32[512]{0:T(512)S(1)}, f32[512,512]{0,1:T(8,128)S(1)}) fusion(s32[512]{0:T(512)S(1)} %broadcast_subtract_fusion.1, bf16[512,4608]{1,0:T(8,128)(2,1)} %param.6, bf16[512,4608]{1,0:T(8,128)(2,1)} %param.5), kind=kOutput, calls=%fused_computation.7 | convolution fusion | flops 2417490944 | bytes 10491904 | tf_op jit(solution)/shard_map/td,vd->tv/dot_general | solution.py:13
  14.8 20.1 %all-reduce = (f32[512]{0:T(512)S(1)}, f32[512]{0:T(512)S(1)}) all-reduce(f32[512]{0:T(512)S(1)} %get-tuple-element.4, f32[512]{0:T(512)S(1)} %get-tuple-element.3), channel_id=1, replica_groups=mesh['dp'=32,'vocab'=8] {'vocab'}, use_global_device_ids=true, to_apply=%region_3.0 | all-reduce | flops 1024 | bytes 8192 | tf_op jit(solution)/shard_map/psum | solution.py:18
  34.9 8.8 %fusion.3 = f32[512,4608]{0,1:T(8,128)} fusion(bf16[512,4608]{1,0:T(8,128)(2,1)} %param.5, f32[512,512]{0,1:T(8,128)S(1)} %get-tuple-element.7, f32[512]{0:T(512)S(1)} %get-tuple-element.6, s32[512]{0:T(512)S(1)} %broadcast_subtract_fusion.1), kind=kOutput, calls=%fused_computation.13 | convolution fusion | flops 2418278400 | bytes 15208448 | tf_op jit(solution)/shard_map/tv,vd->td/dot_general | solution.py:25
  43.7 0.0 copy-start
  43.7 0.0 reduce-scatter.3.cloned.1.call-update
  43.7 0.0 reduce-scatter.5.cloned.1.call-start
  43.7 0.6 copy-done
  44.3 8.6 %fusion.2 = f32[512,4608]{0,1:T(8,128)} fusion(bf16[512,4608]{1,0:T(8,128)(2,1)} %param.6, f32[512,512]{0,1:T(8,128)S(1)} %get-tuple-element.7, f32[512]{0:T(512)S(1)} %get-tuple-element.6, s32[512]{0:T(512)S(1)} %broadcast_subtract_fusion.1), kind=kOutput, calls=%fused_computation.12 | convolution fusion | flops 2418278400 | bytes 15208448 | tf_op jit(solution)/shard_map/tv,td->vd/dot_general | solution.py:27
  53.0 19.7 %all-gather.2.cloned.1.call-done = bf16[512,4608]{0,1:T(8,128)(2,1)} async-done(((bf16[512,576]{0,1:T(8,128)(2,1)}), bf16[512,4608]{0,1:T(8,128)(2,1)}) %all-gather.2.cloned.1.call-update) | async-done | bytes 4718608 | tf_op jit(solution)/shard_map/all_gather | solution.py:31
  72.7 8.9 %convolution_add_fusion = f32[512,4608]{0,1:T(8,128)} fusion(f32[512,4608]{0,1:T(8,128)} %fusion.2, bf16[512,4608]{0,1:T(8,128)(2,1)} %all-gather.2.cloned.1.call-done, s32[512]{0:T(512)S(1)} %broadcast_subtract_fusion), kind=kOutput, calls=%fused_computation | convolution fusion | flops 2418540544 | bytes 23595008 | tf_op jit(solution)/shard_map/dot_general | solution.py:29
  81.6 0.0 reduce-scatter.5.cloned.1.call-update
  81.7 0.6 log_subtract_fusion
  82.2 96.9 %reduce-scatter.3.cloned.1.call-done = f32[512,576]{0,1:T(8,128)} async-done(((f32[512,4608]{0,1:T(8,128)}), f32[512,576]{0,1:T(8,128)}) %reduce-scatter.3.cloned.1.call-update) | async-done | bytes 1179664 | tf_op jit(solution)/shard_map/reduce_scatter | solution.py:26
  179.2 106.2 %reduce-scatter.5.cloned.1.call-done = f32[512,144]{0,1:T(8,128)} async-done(((f32[512,4608]{0,1:T(8,128)}), f32[512,144]{0,1:T(8,128)}) %reduce-scatter.5.cloned.1.call-update) | async-done | bytes 294928 | tf_op jit(solution)/shard_map/reduce_scatter | solution.py:34
  (1 shorter events, 0.0 us)
Async XLA Ops:
  7.2 65.6 %all-gather.2.cloned.1.call-start = ((), (), s32[]{:S(2)}) async-start(), calls=%async_computation.3 | async-start | bytes 5308416 | tf_op jit(solution)/shard_map/all_gather | solution.py:31
  7.9 171.3 %reduce-scatter.3.cloned.1.call-start = ((), (), s32[]{:S(2)}) async-start(), calls=%async_computation.2 | async-start | bytes 10616832 | tf_op jit(solution)/shard_map/reduce_scatter | solution.py:26
  43.7 0.7 copy-start
  43.7 241.7 %reduce-scatter.5.cloned.1.call-start = ((), (), s32[]{:S(2)}) async-start(), calls=%async_computation.4 | async-start | bytes 9732096 | tf_op jit(solution)/shard_map/reduce_scatter | solution.py:34
Sparse Core Ops, SparseCore 0:
  9.8 62.8 all-gather.1
  75.8 103.2 reduce-scatter.2
  183.8 101.5 reduce-scatter.4
where the time goes:
time: 292 us
  waiting for transfers between devices  224 us (77%)
  matrix products  32.4 us (11%)
  blocking collectives  20.1 us (7%)
  between operations  13.8 us (5%)
    reduce_scatter x1, waiting for transfers between devices, per_device(): lax.psum_scatter(tied_part + input_part, 'dp', scatter_dimension=1, tiled...  106 us
    reduce_scatter x1, waiting for transfers between devices, per_device(): lax.psum_scatter(partial_grad, 'vocab', scatter_dimension=1, tiled=True)  96.9 us
    psum x1, blocking collectives, per_device(): lax.psum((jnp.sum(exponent, axis=1), jnp.sum(target_hit * capped, axis=1)...  20.1 us
    all_gather x1, waiting for transfers between devices, per_device(): lax.all_gather(input_grad, 'vocab', axis=1, tiled=True)  19.7 us
    dot_general x1, matrix products, per_device(): jnp.dot(owner_hit, lax.all_gather(input_grad, 'vocab', axis=1, tiled=True...  8.9 us
    dot_general x1, matrix products, per_device(): jnp.einsum('tv,vd->td', scaled, embedding, preferred_element_type=jnp.flo...  8.75 us
    dot_general x1, matrix products, per_device(): jnp.einsum('tv,td->vd', scaled, hidden, preferred_element_type=jnp.float32)  8.64 us
    dot_general x1, matrix products, per_device(): jnp.einsum('td,vd->tv', hidden, embedding, preferred_element_type=jnp.flo...  6.15 us
  transfers between devices with their start and end apart: 3, of which 3 were waited for; matrix products, arithmetic and copies ran while one was open for 12% of the time, Pallas kernels for 0%

commit v1 on v0

v1 whole, which is shorter than its diff:
```python
import jax
import jax.numpy as jnp
from jax import lax
from jax.experimental import pallas as pl
from jax.experimental.pallas import tpu as pltpu
from jax.sharding import PartitionSpec as P

softcap = 30.0
bf16, f16, f32 = jnp.bfloat16, jnp.float16, jnp.float32
NZ, NX, NY = 8, 4, 4
DP = NX * NY * 2
emb_scale = 0.5


def z_shift(d):
    return [(i, (i + d) % NZ) for i in range(NZ)]


def z_xor(d):
    return [(i, i ^ d) for i in range(NZ)]


core_swap = [(i, i ^ 1) for i in range(DP)]


def segment_kernel(x_ref, o_ref):
    groups, rows, lanes = x_ref.shape
    cols = rows // 4 - 2
    r_iota = lax.broadcasted_iota(jnp.int32, (256, lanes), 0).astype(f32)
    q_iota = lax.broadcasted_iota(jnp.int32, (16, lanes), 0).astype(f32)

    def body(g, acc):
        x = x_ref[g].astype(f32)
        left, right = [], []
        for k in range(4):
            base = k * (cols + 2)
            hit = x[base + cols : base + cols + 1] == q_iota
            left.append(
                jnp.concatenate(
                    [jnp.where(hit, x[base + c : base + c + 1], 0.0) for c in range(cols)], axis=0
                ).astype(bf16)
            )
            right.append(jnp.where(x[base + cols + 1 : base + cols + 2] == r_iota, 1.0, 0.0).astype(bf16))
        left = jnp.concatenate(left, axis=1)
        right = jnp.concatenate(right, axis=1)
        return acc + lax.dot_general(left, right, (((1,), (1,)), ((), ())), preferred_element_type=f32)

    acc = lax.fori_loop(0, groups, body, jnp.zeros((cols * 16, 256), f32))
    for c in range(cols):
        for q in range(16):
            o_ref[q // 2, c : c + 1, (q % 2) * 256 : (q % 2 + 1) * 256] = acc[c * 16 + q : c * 16 + q + 1]


def segment_sum(x):
    cols = x.shape[1] // 4 - 2
    return pl.pallas_call(
        segment_kernel,
        out_shape=jax.ShapeDtypeStruct((NZ, cols, 512), f32),
        in_specs=[pl.BlockSpec(memory_space=pltpu.VMEM)],
        out_specs=pl.BlockSpec(memory_space=pltpu.VMEM),
        compiler_params=pltpu.CompilerParams(vmem_limit_bytes=24 * 1024 * 1024),
        cost_estimate=pl.CostEstimate(flops=5_000_000_000, bytes_accessed=2_000_000, transcendentals=0),
    )(x)


same_core = [[2 * chip + c for chip in range(DP // 2)] for c in range(2)]
same_core_parity = [[2 * (2 * b + a) + c for b in range(8)] for a in range(2) for c in range(2)]
MB = 1024 * 1024


def after(x, *others):
    return lax.optimization_barrier((x,) + others)[0]


def hid_kernel(blocks, last, *refs):
    at_ref, emb_ref = refs[:2]
    block_refs = refs[2 : 2 + blocks]
    o_ref = refs[-1]
    rows = block_refs[0].shape[1]
    total = refs[2 + blocks][...] if last else None
    for i, block in enumerate(block_refs):
        term = jnp.dot(block[...], emb_ref[:, at_ref[i]].reshape(rows, -1), preferred_element_type=f32)
        total = term if total is None else total + term
    o_ref[...] = total.T if last else total


def hid_terms(emb_cols, shards, blocks, total=None):
    tokens, piece = blocks[0].shape[0], emb_cols.shape[-1]
    last = total is not None
    at = jnp.stack([s % NZ for s in shards])
    vmem = pl.BlockSpec(memory_space=pltpu.VMEM)
    args = [emb_cols, *blocks] + ([total] if last else [])
    return pl.pallas_call(
        lambda *refs: hid_kernel(len(blocks), last, *refs),
        out_shape=jax.ShapeDtypeStruct((piece, tokens) if last else (tokens, piece), f32),
        in_specs=[pl.BlockSpec(memory_space=pltpu.SMEM)] + [vmem] * len(args),
        out_specs=vmem,
        compiler_params=pltpu.CompilerParams(vmem_limit_bytes=28 * MB),
        cost_estimate=pl.CostEstimate(
            flops=2 * len(blocks) * tokens * tokens * piece, bytes_accessed=8 * MB, transcendentals=0
        ),
    )(at, *args)


def split_kernel(core_ref, x_ref, own_ref, other_ref):
    chips, own_cols, tokens = own_ref.shape
    x = x_ref[...].T.reshape(chips, 2, own_cols, tokens)
    first = core_ref[0] == 0
    own_ref[...] = jnp.where(first, x[:, 0], x[:, 1])
    other_ref[...] = jnp.where(first, x[:, 1], x[:, 0])


def split_hidden(hidden, core):
    tokens, width = hidden.shape
    own_cols = width // DP
    out = jax.ShapeDtypeStruct((DP // 2, own_cols, tokens), hidden.dtype)
    spec = pl.BlockSpec((4, own_cols, tokens), lambda i: (i, 0, 0))
    return pl.pallas_call(
        split_kernel,
        grid=(DP // 8,),
        out_shape=(out, out),
        in_specs=[pl.BlockSpec(memory_space=pltpu.SMEM), pl.BlockSpec((tokens, 8 * own_cols), lambda i: (0, i))],
        out_specs=(spec, spec),
        compiler_params=pltpu.CompilerParams(vmem_limit_bytes=24 * MB),
        cost_estimate=pl.CostEstimate(flops=0, bytes_accessed=9 * MB, transcendentals=0),
    )(core[None], hidden)


def per_device(embedding, hidden, targets, input_ids, input_grad):
    vocab_rows, width = embedding.shape
    tokens = hidden.shape[0]
    z = lax.axis_index("vocab")
    dp = lax.axis_index("dp")
    core, chip = dp % 2, dp // 2
    chips = DP // 2
    offset = z * vocab_rows
    piece = width // NZ
    own_cols = width // DP
    cols = piece // DP

    few = vocab_rows // DP
    emb_few = lax.dynamic_slice(embedding, (dp * few, 0), (few, width))
    emb_few = emb_few.reshape(few, NZ, piece).transpose(1, 0, 2)
    emb_few = lax.all_to_all(emb_few, "vocab", 0, 0, tiled=True)

    logits = jnp.einsum("td,vd->tv", hidden, embedding, preferred_element_type=f32)
    capped = softcap * jnp.tanh(logits / softcap)
    exponent = jnp.exp(capped)
    row_index = jnp.arange(vocab_rows, dtype=jnp.int32)
    target_hit = (row_index[None, :] == (targets - offset)[:, None]).astype(f32)
    stats = jnp.stack([jnp.sum(exponent, axis=1), jnp.sum(target_hit * capped, axis=1)])
    stats1 = stats + lax.ppermute(stats, "vocab", z_xor(1))
    emb_cols = lax.all_gather(after(emb_few, stats), "dp", axis=0, tiled=False)
    grad_t = after(input_grad, stats).T.reshape(2, 2, 8, cols, tokens)
    grad_t = grad_t.transpose(2, 0, 1, 3, 4).reshape(DP, cols, tokens)
    digits = jnp.stack([input_ids // 256, input_ids % 256]).astype(bf16)
    packed = jnp.concatenate([grad_t, jnp.broadcast_to(digits[None], (DP, 2, tokens))], axis=1)
    packed = after(packed, stats1).reshape(DP, cols + 2, 4, 128).transpose(0, 2, 1, 3).reshape(DP, 4 * (cols + 2), 128)
    packed = lax.all_to_all(packed, "dp", 0, 0, tiled=True)

    stats2 = stats1 + lax.ppermute(stats1, "vocab", z_xor(2))

    hid_own, hid_other = split_hidden(after(hidden, stats2), core)
    hid_other = lax.ppermute(hid_other, "dp", core_swap)

    hid_pair = jnp.concatenate([hid_own, hid_other], axis=2)

    stats3 = stats2 + lax.ppermute(stats2, "vocab", z_xor(4))
    denominator, picked = stats3[0], stats3[1]
    token_loss = jnp.log(denominator) - picked
    scaled = (
        (exponent / denominator[:, None] - target_hit) * (1.0 - (capped / softcap) ** 2)
    ).astype(bf16)

    up1, down1 = lax.ppermute(scaled, "vocab", z_shift(1)), lax.ppermute(scaled, "vocab", z_shift(-1))
    scaled_other = lax.ppermute(scaled, "dp", core_swap)

    up2, down2 = lax.ppermute(up1, "vocab", z_shift(1)), lax.ppermute(down1, "vocab", z_shift(-1))

    tied = jnp.einsum("kdt,tv->kdv", hid_pair, jnp.concatenate([scaled, scaled_other]), preferred_element_type=f32)
    tied = after((tied * emb_scale).astype(f16), up1, down1)
    tied = lax.all_to_all(tied, "dp", 0, 0, axis_index_groups=same_core, tiled=True)

    up3, down3 = lax.ppermute(up2, "vocab", z_shift(1)), lax.ppermute(down2, "vocab", z_shift(-1))

    sums = segment_sum(after(packed, up1, down1))
    sums = (sums * emb_scale).astype(f16).reshape(NZ, cols * vocab_rows // 128, 128)
    sums = lax.all_to_all(after(sums, tied), "vocab", 0, 0, tiled=True)

    half = tokens // 2
    up4, down4 = lax.ppermute(up3[:half], "vocab", z_shift(1)), lax.ppermute(down3[half:], "vocab", z_shift(-1))
    sums = lax.all_to_all(sums, "dp", 0, 0, axis_index_groups=same_core_parity, tiled=True)
    sums = sums.reshape(own_cols, vocab_rows)

    hid_sum = hid_terms(
        emb_cols, [z, z + 7, z + 1, z + 6, z + 2], [scaled, up1, down1, up2, down2]
    )
    hidden_grad = hid_terms(
        emb_cols, [z + 5, z + 3, z + 4], [up3, down3, jnp.concatenate([up4, down4], axis=0)], hid_sum
    ).T

    embed_grad = ((jnp.sum(tied.astype(f32), axis=0) + sums.astype(f32)) * (1.0 / emb_scale)).T
    return (token_loss, hidden_grad, embed_grad)


def solution(mesh):
    return jax.shard_map(
        per_device,
        mesh=mesh,
        in_specs=(P("vocab", None), P("dp", None), P("dp"), P("dp"), P("dp", "vocab")),
        out_specs=(P("dp"), P("dp", "vocab"), P("vocab", "dp")),
        check_vma=False,
    )
```

time: 292 us -> 164 us (0.56)
  waiting for transfers between devices: 224 us -> 39.3 us
  starting transfers between devices: 0.12 us -> 54.6 us
  blocking collectives: 20.1 us -> 0 us
  Pallas kernels: 0 us -> 19.3 us
  matrix products: 32.4 us -> 13.9 us
  local copies, waits for them, and re-layouts: 0.61 us -> 13.7 us
  other arithmetic: 1.28 us -> 8.25 us
    reduce_scatter x2 -> x0, waiting for transfers between devices: 203 us -> none  [the longest x1 106 us: per_device(): lax.psum_scatter(tied_part + input_part, 'dp', scatter_dimension=1, tiled...]
    all_to_all x0 -> x5, starting transfers between devices: none -> 34.8 us  [the longest x1 8.47 us: per_device(): emb_few = lax.all_to_all(emb_few, 'vocab', 0, 0, tiled=True)]
    ppermute x0 -> x13, waiting for transfers between devices: none -> 24 us  [the longest x1 9.94 us: per_device(): lax.ppermute(down1, 'vocab', z_shift(-1))]
    psum x1 -> x0, blocking collectives: 20.1 us -> none  [per_device(): lax.psum((jnp.sum(exponent, axis=1), jnp.sum(target_hit * capped, axis=1)...]
    ppermute x0 -> x13, starting transfers between devices: none -> 19.8 us  [the longest x1 4.32 us: per_device(): stats3 = stats2 + lax.ppermute(stats2, 'vocab', z_xor(4))]
    all_gather x1, waiting for transfers between devices: 19.7 us -> 0.01 us  [per_device(): emb_cols = lax.all_gather(after(emb_few, stats), 'dp', axis=0, tiled=False)]
    pallas_call x0 -> x4, Pallas kernels: none -> 19.3 us  [the longest x1 9.54 us: segment_sum(): pl.pallas_call(segment_kernel, out_shape=jax.ShapeDtypeStruct((NZ, cols,...]
    dot_general x4 -> x2, matrix products: 32.4 us -> 13.9 us  [the longest x1 7.45 us: per_device(): jnp.einsum('td,vd->tv', hidden, embedding, preferred_element_type=f32)]
  transfers between devices with their start and end apart: 3 -> 19, of which waited for: 3 -> 10; matrix products, arithmetic and copies ran while one was open for 12% -> 17% of each run, Pallas kernels for 0% -> 8%
where the time goes in v1:
time: 164 us; the launch traced here: 163 us
  starting transfers between devices  54.6 us (33%)
  waiting for transfers between devices  39.3 us (24%)
  Pallas kernels  19.3 us (12%)
  between operations  14.3 us (9%)
  matrix products  13.9 us (8%)
  local copies, waits for them, and re-layouts  13.7 us (8%)
  other arithmetic  8.25 us (5%)
    ppermute x1, waiting for transfers between devices, per_device(): lax.ppermute(down1, 'vocab', z_shift(-1))  9.94 us
    pallas_call x1, Pallas kernels, segment_sum(): pl.pallas_call(segment_kernel, out_shape=jax.ShapeDtypeStruct((NZ, cols,...  9.54 us
    all_to_all x1, starting transfers between devices, per_device(): emb_few = lax.all_to_all(emb_few, 'vocab', 0, 0, tiled=True)  8.47 us
    all_to_all x1, starting transfers between devices, per_device(): packed = lax.all_to_all(packed, 'dp', 0, 0, tiled=True)  7.71 us
    all_to_all x1, waiting for transfers between devices, per_device(): sums = lax.all_to_all(after(sums, tied), 'vocab', 0, 0, tiled=True)  7.62 us
    dot_general x1, matrix products, per_device(): jnp.einsum('td,vd->tv', hidden, embedding, preferred_element_type=f32)  7.45 us
    unnamed x18, local copies, waits for them, and re-layouts  6.92 us
    pallas_call x2, Pallas kernels, hid_terms(): pl.pallas_call(lambda *refs: hid_kernel(len(blocks), last, *refs), out_sh...  6.69 us
  transfers between devices with their start and end apart: 19, of which 10 were waited for; matrix products, arithmetic and copies ran while one was open for 17% of the time, Pallas kernels for 8%

profile of v1, /device:TPU:2, one launch (start us, length us, event | category | flops | bytes accessed | tf_op | source)
XLA Modules:
  0.0 163.3 jit_solution(12897444265512413927)
XLA Ops:
  7.2 0.9 constant_dynamic-slice_fusion
  8.1 0.2 reshape.48
  8.3 0.7 copy.20
  8.9 8.5 %all-to-all-start = ((bf16[8,16,576]{2,1,0:T(8,128)(2,1)}), bf16[8,16,576]{2,1,0:T(8,128)(2,1)S(1)}, u32[]{:S(2)}, u32[]{:S(2)}) async-start(bf16[8,16,576]{2,1,0:T(8,128)(2,1)} %copy.20), calls=%async_computation | async-start | bytes 327680 | tf_op jit(solution)/shard_map/all_to_all | solution.py:144
  17.4 0.0 all-gather.3.cloned.1.call-start
  17.5 0.7 broadcast_subtract_fusion
  18.1 7.5 %exponential_reduce_fusion = (f32[512]{0:T(512)S(1)}, f32[512]{0:T(512)S(1)}, f32[512,512]{1,0:T(8,128)S(1)}) fusion(s32[512]{0:T(512)S(1)} %broadcast_subtract_fusion, bf16[512,4608]{1,0:T(8,128)(2,1)} %x_ref, bf16[512,4608]{1,0:T(8,128)(2,1)} %param.5), kind=kOutput, calls=%fused_computation.14 | convolution fusion | flops 2417490944 | bytes 10491904 | tf_op jit(solution)/shard_map/td,vd->tv/dot_general | solution.py:146
  25.6 1.6 all-to-all-done
  27.2 0.7 copy-done.6
  27.9 0.0 all-gather.3.cloned.1.call-update
  27.9 0.7 collective-permute-start
  28.5 3.0 %collective-permute-done = f32[2,512]{1,0:T(2,128)S(1)} collective-permute-done((f32[2,512]{1,0:T(2,128)S(1)}, f32[2,512]{1,0:T(2,128)S(1)}, u32[]{:S(2)}, u32[]{:S(2)}) %collective-permute-start) | collective-permute-done | bytes 4128 | tf_op jit(solution)/shard_map/ppermute | solution.py:152
  31.6 1.4 collective-permute-start.1
  33.0 3.2 %collective-permute-done.1 = f32[2,512]{1,0:T(2,128)S(1)} collective-permute-done((f32[2,512]{1,0:T(2,128)S(1)}, f32[2,512]{1,0:T(2,128)S(1)}, u32[]{:S(2)}, u32[]{:S(2)}) %collective-permute-start.1) | collective-permute-done | bytes 4128 | tf_op jit(solution)/shard_map/ppermute | solution.py:161
  36.2 0.0 copy-start.2
  36.2 2.3 %copy-done.2 = bf16[512,4608]{1,0:T(8,128)(2,1)S(1)} copy-done((bf16[512,4608]{1,0:T(8,128)(2,1)S(1)}, bf16[512,4608]{1,0:T(8,128)(2,1)}, u32[]{:S(2)}) %copy-start.2) | copy-done | bytes 4718616
  38.6 3.1 %shard_map.78 = (bf16[16,144,512]{2,1,0:T(8,128)(2,1)S(1)}, bf16[16,144,512]{2,1,0:T(8,128)(2,1)}) custom-call(s32[1]{0:T(128)} %bitcast.15.core_ref, bf16[512,4608]{1,0:T(8,128)(2,1)S(1)} %copy-done.2), custom_call_target="tpu_custom_call" | custom-call | bytes 9437184 | tf_op jit(solution)/shard_map/pallas_call | solution.py:118
  41.7 1.4 copy-done.5
  43.1 0.0 collective-permute-start.11
  43.1 4.3 %collective-permute-start.2 = (f32[2,512]{1,0:T(2,128)S(1)}, f32[2,512]{1,0:T(2,128)S(1)}, u32[]{:S(2)}, u32[]{:S(2)}) collective-permute-start(f32[2,512]{1,0:T(2,128)S(1)} %fusion.17), channel_id=1, source_target_pairs={{0,4},{1,5},{2,6},{3,7},{4,0},{5,1},{6,2},{7,3},{8,12},{9,13},{10,... | collective-permute-start | bytes 12296 | tf_op jit(solution)/shard_map/ppermute | solution.py:168
  47.4 0.2 reshape.49
  47.6 0.6 copy.21
  48.2 0.2 reshape.50
  48.4 2.2 %collective-permute-done.2 = f32[2,512]{1,0:T(2,128)S(1)} collective-permute-done((f32[2,512]{1,0:T(2,128)S(1)}, f32[2,512]{1,0:T(2,128)S(1)}, u32[]{:S(2)}, u32[]{:S(2)}) %collective-permute-start.2) | collective-permute-done | bytes 4128 | tf_op jit(solution)/shard_map/ppermute | solution.py:168
  50.6 0.4 multiply_convert_fusion.1.refs_2_
  51.0 0.1 collective-permute-start.12
  51.2 0.1 pad_maximum_fusion
  51.3 0.2 reshape.51
  51.4 0.1 copy.22
  51.6 1.1 copy.23
  52.6 7.7 %all-to-all-start.2 = ((bf16[32,80,128]{2,1,0:T(8,128)(2,1)}), bf16[32,80,128]{2,1,0:T(8,128)(2,1)S(1)}, u32[]{:S(2)}, u32[]{:S(2)}) async-start(bf16[32,80,128]{2,1,0:T(8,128)(2,1)} %copy.23), calls=%async_computation.2 | async-start | bytes 1310720 | tf_op jit(solution)/shard_map/all_to_all | solution.py:159
  60.4 0.6 collective-permute-start.3
  61.0 2.7 %collective-permute-start.6 = (bf16[512,512]{1,0:T(8,128)(2,1)S(1)}, bf16[512,512]{1,0:T(8,128)(2,1)S(1)}, u32[]{:S(2)}, u32[]{:S(2)}) collective-permute-start(bf16[512,512]{1,0:T(8,128)(2,1)S(1)} %multiply_convert_fusion.1.refs_2_), channel_id=1, source_target_pairs={{0,7},{1,0},{2,1},{3,2},{4,3},{5,4},{6,5},{7,6},{8,15},{9,8},{10,9... | collective-permute-start | bytes 1572872 | tf_op jit(solution)/shard_map/ppermute | solution.py:175
  63.7 0.0 collective-permute-done.12
  63.7 0.0 collective-permute-done.11
  63.7 6.5 %multiply_convert_fusion = f16[16,144,512]{2,1,0:T(8,128)(2,1)} fusion(bf16[16,144,512]{2,1,0:T(8,128)(2,1)} %collective-permute-done.11, bf16[16,144,512]{2,1,0:T(8,128)(2,1)} %copy-done.5, bf16[512,512]{1,0:T(8,128)(2,1)S(1)} %collective-permute-done.12, bf16[512,512]{1,0:T(8,128)(2,1)S(1)} %multiply_convert_fusion.1.refs_2_), kind=kOutput, calls=%fused_computation.5 | convolution fusion | flops 2429812736 | bytes 8126464 | tf_op jit(solution)/shard_map/kdt,tv->kdv/dot_general | solution.py:180
  70.2 5.5 %collective-permute-done.3.refs_3_ = bf16[512,512]{1,0:T(8,128)(2,1)S(1)} collective-permute-done((bf16[512,512]{1,0:T(8,128)(2,1)S(1)}, bf16[512,512]{1,0:T(8,128)(2,1)S(1)}, u32[]{:S(2)}, u32[]{:S(2)}) %collective-permute-start.3) | collective-permute-done | bytes 524320 | tf_op jit(solution)/shard_map/ppermute | solution.py:175
  75.6 0.0 collective-permute-done.6.refs_4_
  75.6 0.6 all-to-all-done.2.x_ref
  76.2 6.7 %all-to-all-start.1 = ((f16[16,144,512]{2,1,0:T(8,128)(2,1)}), f16[16,144,512]{2,1,0:T(8,128)(2,1)}, u32[]{:S(2)}, u32[]{:S(2)}) async-start(f16[16,144,512]{2,1,0:T(8,128)(2,1)} %multiply_convert_fusion), calls=%async_computation.1 | async-start | bytes 4718592 | tf_op jit(solution)/shard_map/all_to_all | solution.py:182
  82.9 2.9 %collective-permute-start.7 = (bf16[512,512]{1,0:T(8,128)(2,1)S(1)}, bf16[512,512]{1,0:T(8,128)(2,1)}, u32[]{:S(2)}, u32[]{:S(2)}) collective-permute-start(bf16[512,512]{1,0:T(8,128)(2,1)S(1)} %collective-permute-done.6.refs_4_), channel_id=1, source_target_pairs={{0,7},{1,0},{2,1},{3,2},{4,3},{5,4},{6,5},{7,6},{8,15},{9,8},{10,9... | collective-permute-start | bytes 1572872 | tf_op jit(solution)/shard_map/ppermute | solution.py:178
  85.8 0.0 collective-permute-start.4
  85.8 9.9 %collective-permute-done.7.refs_6_ = bf16[512,512]{1,0:T(8,128)(2,1)} collective-permute-done((bf16[512,512]{1,0:T(8,128)(2,1)S(1)}, bf16[512,512]{1,0:T(8,128)(2,1)}, u32[]{:S(2)}, u32[]{:S(2)}) %collective-permute-start.7) | collective-permute-done | bytes 524320 | tf_op jit(solution)/shard_map/ppermute | solution.py:178
  95.8 3.6 %collective-permute-start.8 = (bf16[512,512]{1,0:T(8,128)(2,1)}, bf16[512,512]{1,0:T(8,128)(2,1)S(1)}, u32[]{:S(2)}, u32[]{:S(2)}) collective-permute-start(bf16[512,512]{1,0:T(8,128)(2,1)} %collective-permute-done.7.refs_6_), channel_id=1, source_target_pairs={{0,7},{1,0},{2,1},{3,2},{4,3},{5,4},{6,5},{7,6},{8,15},{9,8},{10,9... | collective-permute-start | bytes 1572872 | tf_op jit(solution)/shard_map/ppermute | solution.py:184
  99.4 0.1 pad_add_fusion.refs_0_
  99.5 0.1 stack.60.refs_0_
  99.6 9.5 %shard_map.79 = f32[8,18,512]{2,1,0:T(8,128)S(1)} custom-call(bf16[32,80,128]{2,1,0:T(8,128)(2,1)S(1)} %all-to-all-done.2.x_ref), custom_call_target="tpu_custom_call" | custom-call | flops 5000000000 | bytes 2000000 | tf_op jit(solution)/shard_map/pallas_call | solution.py:56
  109.2 3.3 %collective-permute-start.10 = (bf16[256,512]{1,0:T(8,128)(2,1)S(1)}, bf16[256,512]{1,0:T(8,128)(2,1)}, u32[]{:S(2)}, u32[]{:S(2)}) collective-permute-start(bf16[256,512]{1,0:T(8,128)(2,1)S(1)} %slice.19), channel_id=1, source_target_pairs={{0,7},{1,0},{2,1},{3,2},{4,3},{5,4},{6,5},{7,6},{8,15},{9,8},{10,9... | collective-permute-start | bytes 786440 | tf_op jit(solution)/shard_map/ppermute | solution.py:191
  112.5 0.1 collective-permute-start.9
  112.7 0.8 reshape.53
  113.4 6.2 %all-to-all-start.3 = ((f16[8,72,128]{2,1,0:T(8,128)(2,1)}), f16[8,72,128]{2,1,0:T(8,128)(2,1)}, u32[]{:S(2)}, u32[]{:S(2)}) async-start(f16[8,72,128]{2,1,0:T(8,128)(2,1)} %reshape.53), calls=%async_computation.3 | async-start | bytes 294912 | tf_op jit(solution)/shard_map/all_to_all | solution.py:188
  119.6 0.6 log_subtract_fusion
  120.2 0.1 collective-permute-done.9
  120.3 1.1 pad_maximum_fusion.1.refs_4_
  121.4 7.6 %all-to-all-done.3 = f16[8,72,128]{2,1,0:T(8,128)(2,1)} async-done(((f16[8,72,128]{2,1,0:T(8,128)(2,1)}), f16[8,72,128]{2,1,0:T(8,128)(2,1)}, u32[]{:S(2)}, u32[]{:S(2)}) %all-to-all-start.3) | async-done | bytes 147488 | tf_op jit(solution)/shard_map/all_to_all | solution.py:188
  129.0 5.8 %all-to-all-start.4 = ((f16[8,72,128]{2,1,0:T(8,128)(2,1)}), f16[8,72,128]{2,1,0:T(8,128)(2,1)S(1)}, u32[]{:S(2)}, u32[]{:S(2)}) async-start(f16[8,72,128]{2,1,0:T(8,128)(2,1)} %all-to-all-done.3), calls=%async_computation.4 | async-start | bytes 294912 | tf_op jit(solution)/shard_map/all_to_all | solution.py:192
  134.7 2.7 %convert_reduce_fusion = f32[144,512]{1,0:T(8,128)} fusion(f16[16,144,512]{2,1,0:T(8,128)(2,1)} %all-to-all-done.1), kind=kLoop, calls=%fused_computation.4 | loop fusion | flops 2285568 | bytes 2654208 | tf_op jit(solution)/shard_map/reduce_sum | solution.py:202
  137.4 5.5 %all-to-all-done.4 = f16[8,72,128]{2,1,0:T(8,128)(2,1)S(1)} async-done(((f16[8,72,128]{2,1,0:T(8,128)(2,1)}), f16[8,72,128]{2,1,0:T(8,128)(2,1)S(1)}, u32[]{:S(2)}, u32[]{:S(2)}) %all-to-all-start.4) | async-done | bytes 147488 | tf_op jit(solution)/shard_map/all_to_all | solution.py:192
  143.0 0.7 convert_element_type.33
  143.7 1.7 %reshape.54 = f32[144,512]{1,0:T(8,128)} reshape(f32[8,72,128]{2,1,0:T(8,128)} %convert_element_type.33) | data formatting | bytes 589824 | tf_op jit(solution)/shard_map/convert_element_type | solution.py:202
  145.5 1.8 %multiply_bitcast_fusion = f32[512,144]{0,1:T(8,128)} fusion(f32[144,512]{1,0:T(8,128)} %convert_reduce_fusion, f32[144,512]{1,0:T(8,128)} %reshape.54), kind=kLoop, calls=%fused_computation.18 | loop fusion | flops 147456 | bytes 884736 | tf_op jit(solution)/shard_map/transpose | solution.py:202
  147.3 2.5 %copy-done = bf16[256,16,576]{2,1,0:T(8,128)(2,1)S(1)} copy-done((bf16[256,16,576]{2,1,0:T(8,128)(2,1)S(1)}, bf16[256,16,576]{2,1,0:T(8,128)(2,1)}, u32[]{:S(2)}) %copy-start) | copy-done | bytes 4718616
  149.8 3.6 %shard_map.76.refs_5_ = f32[512,576]{1,0:T(8,128)S(1)} custom-call(s32[5]{0:T(128)S(1)} %stack.60.refs_0_, bf16[32,8,16,576]{3,2,1,0:T(8,128)(2,1)S(1)} %bitcast.31, bf16[512,512]{1,0:T(8,128)(2,1)S(1)} %multiply_convert_fusion.1.refs_2_, bf16[512,512]{1,0:T(8,128)(2,1)S(1)} %collective-permute-done.3.refs_3_, bf16[512,512]{1,0:T(8,128)(2,1)S(1)} %copy-done.4, ...), custom_call_target="tpu_custom_call" | custom-call | flops 1509949440 | bytes 8388608 | tf_op jit(solution)/shard_map/pallas_call | solution.py:93
  153.4 3.1 %shard_map.77 = f32[576,512]{1,0:T(8,128)} custom-call(s32[3]{0:T(128)S(1)} %pad_add_fusion.refs_0_, bf16[32,8,16,576]{3,2,1,0:T(8,128)(2,1)S(1)} %bitcast.32, bf16[512,512]{1,0:T(8,128)(2,1)S(1)} %collective-permute-done.5.refs_2_, bf16[512,512]{1,0:T(8,128)(2,1)S(1)} %collective-permute-done.8.refs_3_, bf16[512,512]{1,0:T(8,128)(2,1)S(1)} %pad_maximum_fusion.1.refs_4_, ...), custom_call_target="tpu_custom_call" | custom-call | flops 905969664 | bytes 8388608 | tf_op jit(solution)/shard_map/pallas_call | solution.py:93
  (33 shorter events, 0.2 us)
Async XLA Ops:
  8.9 18.2 %all-to-all-start = ((bf16[8,16,576]{2,1,0:T(8,128)(2,1)}), bf16[8,16,576]{2,1,0:T(8,128)(2,1)S(1)}, u32[]{:S(2)}, u32[]{:S(2)}) async-start(bf16[8,16,576]{2,1,0:T(8,128)(2,1)} %copy.20), calls=%async_computation | async-start | bytes 327680 | tf_op jit(solution)/shard_map/all_to_all | solution.py:144
  17.4 129.9 %all-gather.3.cloned.1.call-start = ((), (), s32[]{:S(2)}) async-start(), calls=%async_computation.5 | async-start | bytes 5406720 | tf_op jit(solution)/shard_map/all_gather | solution.py:153
  18.1 29.2 %copy-start.7 = (bf16[512,576]{0,1:T(8,128)(2,1)S(1)}, bf16[512,576]{0,1:T(8,128)(2,1)}, u32[]{:S(2)}) copy-start(bf16[512,576]{0,1:T(8,128)(2,1)} %param.9) | copy-start | bytes 1769476
  27.2 0.7 copy-start.6
  27.9 3.7 %collective-permute-start = (f32[2,512]{1,0:T(2,128)S(1)}, f32[2,512]{1,0:T(2,128)S(1)}, u32[]{:S(2)}, u32[]{:S(2)}) collective-permute-start(f32[2,512]{1,0:T(2,128)S(1)} %pad_maximum_fusion.2), channel_id=1, source_target_pairs={{0,1},{1,0},{2,3},{3,2},{4,5},{5,4},{6,7},{7,6},{8,9},{9,8},{10,11... | collective-permute-start | bytes 12296 | tf_op jit(solution)/shard_map/ppermute | solution.py:152
  31.6 4.6 %collective-permute-start.1 = (f32[2,512]{1,0:T(2,128)S(1)}, f32[2,512]{1,0:T(2,128)S(1)}, u32[]{:S(2)}, u32[]{:S(2)}) collective-permute-start(f32[2,512]{1,0:T(2,128)S(1)} %fusion.13), channel_id=1, source_target_pairs={{0,2},{1,3},{2,0},{3,1},{4,6},{5,7},{6,4},{7,5},{8,10},{9,11},{10,... | collective-permute-start | bytes 12296 | tf_op jit(solution)/shard_map/ppermute | solution.py:161
  36.2 2.3 %copy-start.2 = (bf16[512,4608]{1,0:T(8,128)(2,1)S(1)}, bf16[512,4608]{1,0:T(8,128)(2,1)}, u32[]{:S(2)}) copy-start(bf16[512,4608]{1,0:T(8,128)(2,1)} %x_ref) | copy-start | bytes 14155780
  38.6 12.6 %copy-start.8 = (s32[512]{0:T(512)S(1)}, s32[512]{0:T(512)}, u32[]{:S(2)}) copy-start(s32[512]{0:T(512)} %param.8) | copy-start | bytes 6148
  41.7 1.4 copy-start.5
  43.1 20.6 %collective-permute-start.11 = (bf16[16,144,512]{2,1,0:T(8,128)(2,1)}, bf16[16,144,512]{2,1,0:T(8,128)(2,1)}, u32[]{:S(2)}, u32[]{:S(2)}) collective-permute-start(bf16[16,144,512]{2,1,0:T(8,128)(2,1)} %get-tuple-element.15), channel_id=1, source_target_pairs={{0,8},{8,0},{16,24},{24,16},{32,40},{40,32},{48,56},{56,48},{64,72... | collective-permute-start | bytes 7077896 | tf_op jit(solution)/shard_map/ppermute | solution.py:164
  43.1 7.5 %collective-permute-start.2 = (f32[2,512]{1,0:T(2,128)S(1)}, f32[2,512]{1,0:T(2,128)S(1)}, u32[]{:S(2)}, u32[]{:S(2)}) collective-permute-start(f32[2,512]{1,0:T(2,128)S(1)} %fusion.17), channel_id=1, source_target_pairs={{0,4},{1,5},{2,6},{3,7},{4,0},{5,1},{6,2},{7,3},{8,12},{9,13},{10,... | collective-permute-start | bytes 12296 | tf_op jit(solution)/shard_map/ppermute | solution.py:168
  51.0 12.7 %collective-permute-start.12 = (bf16[512,512]{1,0:T(8,128)(2,1)S(1)}, bf16[512,512]{1,0:T(8,128)(2,1)S(1)}, u32[]{:S(2)}, u32[]{:S(2)}) collective-permute-start(bf16[512,512]{1,0:T(8,128)(2,1)S(1)} %multiply_convert_fusion.1.refs_2_), channel_id=1, source_target_pairs={{0,8},{8,0},{16,24},{24,16},{32,40},{40,32},{48,56},{56,48},{64,72... | collective-permute-start | bytes 1572872 | tf_op jit(solution)/shard_map/ppermute | solution.py:176
  52.6 23.6 %all-to-all-start.2 = ((bf16[32,80,128]{2,1,0:T(8,128)(2,1)}), bf16[32,80,128]{2,1,0:T(8,128)(2,1)S(1)}, u32[]{:S(2)}, u32[]{:S(2)}) async-start(bf16[32,80,128]{2,1,0:T(8,128)(2,1)} %copy.23), calls=%async_computation.2 | async-start | bytes 1310720 | tf_op jit(solution)/shard_map/all_to_all | solution.py:159
  60.4 15.3 %collective-permute-start.3 = (bf16[512,512]{1,0:T(8,128)(2,1)S(1)}, bf16[512,512]{1,0:T(8,128)(2,1)S(1)}, u32[]{:S(2)}, u32[]{:S(2)}) collective-permute-start(bf16[512,512]{1,0:T(8,128)(2,1)S(1)} %multiply_convert_fusion.1.refs_2_), channel_id=1, source_target_pairs={{0,1},{1,2},{2,3},{3,4},{4,5},{5,6},{6,7},{7,0},{8,9},{9,10},{10,1... | collective-permute-start | bytes 1572872 | tf_op jit(solution)/shard_map/ppermute | solution.py:175
  61.0 14.7 %collective-permute-start.6 = (bf16[512,512]{1,0:T(8,128)(2,1)S(1)}, bf16[512,512]{1,0:T(8,128)(2,1)S(1)}, u32[]{:S(2)}, u32[]{:S(2)}) collective-permute-start(bf16[512,512]{1,0:T(8,128)(2,1)S(1)} %multiply_convert_fusion.1.refs_2_), channel_id=1, source_target_pairs={{0,7},{1,0},{2,1},{3,2},{4,3},{5,4},{6,5},{7,6},{8,15},{9,8},{10,9... | collective-permute-start | bytes 1572872 | tf_op jit(solution)/shard_map/ppermute | solution.py:175
  75.6 33.5 %copy-start.3 = (bf16[512,512]{1,0:T(8,128)(2,1)}, bf16[512,512]{1,0:T(8,128)(2,1)S(1)}, u32[]{:S(2)}) copy-start(bf16[512,512]{1,0:T(8,128)(2,1)S(1)} %collective-permute-done.6.refs_4_) | copy-start | bytes 1572868
  76.2 37.2 %all-to-all-start.1 = ((f16[16,144,512]{2,1,0:T(8,128)(2,1)}), f16[16,144,512]{2,1,0:T(8,128)(2,1)}, u32[]{:S(2)}, u32[]{:S(2)}) async-start(f16[16,144,512]{2,1,0:T(8,128)(2,1)} %multiply_convert_fusion), calls=%async_computation.1 | async-start | bytes 4718592 | tf_op jit(solution)/shard_map/all_to_all | solution.py:182
  82.9 12.9 %collective-permute-start.7 = (bf16[512,512]{1,0:T(8,128)(2,1)S(1)}, bf16[512,512]{1,0:T(8,128)(2,1)}, u32[]{:S(2)}, u32[]{:S(2)}) collective-permute-start(bf16[512,512]{1,0:T(8,128)(2,1)S(1)} %collective-permute-done.6.refs_4_), channel_id=1, source_target_pairs={{0,7},{1,0},{2,1},{3,2},{4,3},{5,4},{6,5},{7,6},{8,15},{9,8},{10,9... | collective-permute-start | bytes 1572872 | tf_op jit(solution)/shard_map/ppermute | solution.py:178
  85.8 13.6 %collective-permute-start.4 = (bf16[512,512]{1,0:T(8,128)(2,1)S(1)}, bf16[512,512]{1,0:T(8,128)(2,1)}, u32[]{:S(2)}, u32[]{:S(2)}) collective-permute-start(bf16[512,512]{1,0:T(8,128)(2,1)S(1)} %collective-permute-done.3.refs_3_), channel_id=1, source_target_pairs={{0,1},{1,2},{2,3},{3,4},{4,5},{5,6},{6,7},{7,0},{8,9},{9,10},{10,1... | collective-permute-start | bytes 1572872 | tf_op jit(solution)/shard_map/ppermute | solution.py:178
  95.8 13.4 %collective-permute-start.8 = (bf16[512,512]{1,0:T(8,128)(2,1)}, bf16[512,512]{1,0:T(8,128)(2,1)S(1)}, u32[]{:S(2)}, u32[]{:S(2)}) collective-permute-start(bf16[512,512]{1,0:T(8,128)(2,1)} %collective-permute-done.7.refs_6_), channel_id=1, source_target_pairs={{0,7},{1,0},{2,1},{3,2},{4,3},{5,4},{6,5},{7,6},{8,15},{9,8},{10,9... | collective-permute-start | bytes 1572872 | tf_op jit(solution)/shard_map/ppermute | solution.py:184
  99.4 13.1 %collective-permute-start.5 = (bf16[512,512]{1,0:T(8,128)(2,1)}, bf16[512,512]{1,0:T(8,128)(2,1)S(1)}, u32[]{:S(2)}, u32[]{:S(2)}) collective-permute-start(bf16[512,512]{1,0:T(8,128)(2,1)} %collective-permute-done.4.refs_5_), channel_id=1, source_target_pairs={{0,1},{1,2},{2,3},{3,4},{4,5},{5,6},{6,7},{7,0},{8,9},{9,10},{10,1... | collective-permute-start | bytes 1572872 | tf_op jit(solution)/shard_map/ppermute | solution.py:184
  109.1 38.1 %copy-start.4 = (bf16[512,512]{1,0:T(8,128)(2,1)S(1)}, bf16[512,512]{1,0:T(8,128)(2,1)}, u32[]{:S(2)}) copy-start(bf16[512,512]{1,0:T(8,128)(2,1)} %copy-done.3) | copy-start | bytes 1572868
  109.2 11.0 %collective-permute-start.10 = (bf16[256,512]{1,0:T(8,128)(2,1)S(1)}, bf16[256,512]{1,0:T(8,128)(2,1)}, u32[]{:S(2)}, u32[]{:S(2)}) collective-permute-start(bf16[256,512]{1,0:T(8,128)(2,1)S(1)} %slice.19), channel_id=1, source_target_pairs={{0,7},{1,0},{2,1},{3,2},{4,3},{5,4},{6,5},{7,6},{8,15},{9,8},{10,9... | collective-permute-start | bytes 786440 | tf_op jit(solution)/shard_map/ppermute | solution.py:191
  112.5 7.8 %collective-permute-start.9 = (bf16[256,512]{1,0:T(8,128)(2,1)S(1)}, bf16[256,512]{1,0:T(8,128)(2,1)}, u32[]{:S(2)}, u32[]{:S(2)}) collective-permute-start(bf16[256,512]{1,0:T(8,128)(2,1)S(1)} %slice.18), channel_id=1, source_target_pairs={{0,1},{1,2},{2,3},{3,4},{4,5},{5,6},{6,7},{7,0},{8,9},{9,10},{10,1... | collective-permute-start | bytes 786440 | tf_op jit(solution)/shard_map/ppermute | solution.py:191
  113.4 15.5 %all-to-all-start.3 = ((f16[8,72,128]{2,1,0:T(8,128)(2,1)}), f16[8,72,128]{2,1,0:T(8,128)(2,1)}, u32[]{:S(2)}, u32[]{:S(2)}) async-start(f16[8,72,128]{2,1,0:T(8,128)(2,1)} %reshape.53), calls=%async_computation.3 | async-start | bytes 294912 | tf_op jit(solution)/shard_map/all_to_all | solution.py:188
  129.0 14.0 %all-to-all-start.4 = ((f16[8,72,128]{2,1,0:T(8,128)(2,1)}), f16[8,72,128]{2,1,0:T(8,128)(2,1)S(1)}, u32[]{:S(2)}, u32[]{:S(2)}) async-start(f16[8,72,128]{2,1,0:T(8,128)(2,1)} %all-to-all-done.3), calls=%async_computation.4 | async-start | bytes 294912 | tf_op jit(solution)/shard_map/all_to_all | solution.py:192
  147.3 2.5 %copy-start = (bf16[256,16,576]{2,1,0:T(8,128)(2,1)S(1)}, bf16[256,16,576]{2,1,0:T(8,128)(2,1)}, u32[]{:S(2)}) copy-start(bf16[256,16,576]{2,1,0:T(8,128)(2,1)} %all-gather.3.cloned.1.call-done) | copy-start | bytes 14155780
  149.8 3.6 %copy-start.1 = (bf16[256,16,576]{2,1,0:T(8,128)(2,1)S(1)}, bf16[256,16,576]{2,1,0:T(8,128)(2,1)}, u32[]{:S(2)}) copy-start(bf16[256,16,576]{2,1,0:T(8,128)(2,1)} %all-gather.3.cloned.1.call-done) | copy-start | bytes 14155780
Sparse Core Ops, SparseCore 0:
  28.0 56.1 all-gather.2

commit v2 on v1

--- a/solution.py
+++ b/solution.py
@@ -29,23 +29,24 @@
     r_iota = lax.broadcasted_iota(jnp.int32, (256, lanes), 0).astype(f32)
     q_iota = lax.broadcasted_iota(jnp.int32, (16, lanes), 0).astype(f32)
 
-    def body(g, acc):
-        x = x_ref[g].astype(f32)
+    def body(step, acc):
         left, right = [], []
-        for k in range(4):
-            base = k * (cols + 2)
-            hit = x[base + cols : base + cols + 1] == q_iota
-            left.append(
-                jnp.concatenate(
-                    [jnp.where(hit, x[base + c : base + c + 1], 0.0) for c in range(cols)], axis=0
-                ).astype(bf16)
-            )
-            right.append(jnp.where(x[base + cols + 1 : base + cols + 2] == r_iota, 1.0, 0.0).astype(bf16))
+        for n in range(4):
+            x = x_ref[4 * step + n].astype(f32)
+            for k in range(4):
+                base = k * (cols + 2)
+                hit = x[base + cols : base + cols + 1] == q_iota
+                left.append(
+                    jnp.concatenate(
+                        [jnp.where(hit, x[base + c : base + c + 1], 0.0) for c in range(cols)], axis=0
+                    ).astype(bf16)
+                )
+                right.append(jnp.where(x[base + cols + 1 : base + cols + 2] == r_iota, 1.0, 0.0).astype(bf16))
         left = jnp.concatenate(left, axis=1)
         right = jnp.concatenate(right, axis=1)
         return acc + lax.dot_general(left, right, (((1,), (1,)), ((), ())), preferred_element_type=f32)
 
-    acc = lax.fori_loop(0, groups, body, jnp.zeros((cols * 16, 256), f32))
+    acc = lax.fori_loop(0, groups // 4, body, jnp.zeros((cols * 16, 256), f32))
     for c in range(cols):
         for q in range(16):
             o_ref[q // 2, c : c + 1, (q % 2) * 256 : (q % 2 + 1) * 256] = acc[c * 16 + q : c * 16 + q + 1]
@@ -64,7 +65,6 @@
 
 
 same_core = [[2 * chip + c for chip in range(DP // 2)] for c in range(2)]
-same_core_parity = [[2 * (2 * b + a) + c for b in range(8)] for a in range(2) for c in range(2)]
 MB = 1024 * 1024
 
 
@@ -100,6 +100,34 @@
             flops=2 * len(blocks) * tokens * tokens * piece, bytes_accessed=8 * MB, transcendentals=0
         ),
     )(at, *args)
+
+
+def pack_kernel(grad_ref, ids_ref, o_ref):
+    cols = o_ref.shape[1] // 4 - 2
+    grad = grad_ref[...].astype(f32)
+    ids = ids_ref[...]
+    digits = [(ids // 256).astype(f32), (ids % 256).astype(f32)]
+    for device in range(DP):
+        b, a, c = device // 4, device // 2 % 2, device % 2
+        base = ((a * 2 + c) * 8 + b) * cols
+        rows = []
+        for k in range(4):
+            lanes = slice(k * 128, (k + 1) * 128)
+            rows += [grad[base : base + cols, lanes]] + [d[:, lanes] for d in digits]
+        o_ref[device] = jnp.concatenate(rows, axis=0).astype(bf16)
+
+
+def pack_input(grad_t, ids):
+    piece, tokens = grad_t.shape
+    vmem = pl.BlockSpec(memory_space=pltpu.VMEM)
+    return pl.pallas_call(
+        pack_kernel,
+        out_shape=jax.ShapeDtypeStruct((DP, 4 * (piece // DP + 2), tokens // 4), bf16),
+        in_specs=[vmem, vmem],
+        out_specs=vmem,
+        compiler_params=pltpu.CompilerParams(vmem_limit_bytes=16 * MB),
+        cost_estimate=pl.CostEstimate(flops=0, bytes_accessed=2 * MB, transcendentals=0),
+    )(grad_t, ids.reshape(1, tokens))
 
 
 def split_kernel(core_ref, x_ref, own_ref, other_ref):
@@ -151,21 +179,13 @@
     stats = jnp.stack([jnp.sum(exponent, axis=1), jnp.sum(target_hit * capped, axis=1)])
     stats1 = stats + lax.ppermute(stats, "vocab", z_xor(1))
     emb_cols = lax.all_gather(after(emb_few, stats), "dp", axis=0, tiled=False)
-    grad_t = after(input_grad, stats).T.reshape(2, 2, 8, cols, tokens)
-    grad_t = grad_t.transpose(2, 0, 1, 3, 4).reshape(DP, cols, tokens)
-    digits = jnp.stack([input_ids // 256, input_ids % 256]).astype(bf16)
-    packed = jnp.concatenate([grad_t, jnp.broadcast_to(digits[None], (DP, 2, tokens))], axis=1)
-    packed = after(packed, stats1).reshape(DP, cols + 2, 4, 128).transpose(0, 2, 1, 3).reshape(DP, 4 * (cols + 2), 128)
+    packed = pack_input(after(input_grad, stats).T, input_ids)
+    stats1 = after(stats1, packed)
+    stats2 = stats1 + lax.ppermute(stats1, "vocab", z_xor(2))
     packed = lax.all_to_all(packed, "dp", 0, 0, tiled=True)
 
-    stats2 = stats1 + lax.ppermute(stats1, "vocab", z_xor(2))
-
-    hid_own, hid_other = split_hidden(after(hidden, stats2), core)
-    hid_other = lax.ppermute(hid_other, "dp", core_swap)
-
-    hid_pair = jnp.concatenate([hid_own, hid_other], axis=2)
-
     stats3 = stats2 + lax.ppermute(stats2, "vocab", z_xor(4))
+    stats3 = after(stats3, packed)
     denominator, picked = stats3[0], stats3[1]
     token_loss = jnp.log(denominator) - picked
     scaled = (
@@ -175,23 +195,32 @@
     up1, down1 = lax.ppermute(scaled, "vocab", z_shift(1)), lax.ppermute(scaled, "vocab", z_shift(-1))
     scaled_other = lax.ppermute(scaled, "dp", core_swap)
 
+    hid_own, hid_other = split_hidden(after(hidden, stats2), core)
+    hid_other = lax.ppermute(hid_other, "dp", core_swap)
+    row = lax.broadcasted_iota(jnp.int32, (chips * own_cols, 2 * NZ * cols), 0)
+    term = lax.broadcasted_iota(jnp.int32, (chips * own_cols, 2 * NZ * cols), 1) % (NZ * cols)
+    place = (2 * (term // cols) + chip % 2) * own_cols + chip // 2 * cols + term % cols
+    place = jnp.where(row == place, 1.0 / emb_scale, 0.0).astype(bf16).reshape(chips, own_cols, 2 * NZ * cols)
+    hid_pair = jnp.concatenate([hid_own, hid_other, place], axis=2)
+
     up2, down2 = lax.ppermute(up1, "vocab", z_shift(1)), lax.ppermute(down1, "vocab", z_shift(-1))
-
-    tied = jnp.einsum("kdt,tv->kdv", hid_pair, jnp.concatenate([scaled, scaled_other]), preferred_element_type=f32)
-    tied = after((tied * emb_scale).astype(f16), up1, down1)
-    tied = lax.all_to_all(tied, "dp", 0, 0, axis_index_groups=same_core, tiled=True)
-
-    up3, down3 = lax.ppermute(up2, "vocab", z_shift(1)), lax.ppermute(down2, "vocab", z_shift(-1))
 
     sums = segment_sum(after(packed, up1, down1))
     sums = (sums * emb_scale).astype(f16).reshape(NZ, cols * vocab_rows // 128, 128)
-    sums = lax.all_to_all(after(sums, tied), "vocab", 0, 0, tiled=True)
+    sums = lax.all_to_all(after(sums, up1, down1), "vocab", 0, 0, tiled=True).reshape(NZ * cols, vocab_rows)
+    sums_high = sums.astype(bf16)
+    sums_low = (sums.astype(f32) - sums_high.astype(f32)).astype(bf16)
+
+    up3, down3 = lax.ppermute(up2, "vocab", z_shift(1)), lax.ppermute(down2, "vocab", z_shift(-1))
+
+    sums_high = after(sums_high, up2, down2)
+    terms = jnp.concatenate([scaled, scaled_other, sums_high, sums_low])
+    tied = jnp.einsum("kdt,tv->kdv", hid_pair, terms, preferred_element_type=f32)
+    tied = (tied * emb_scale).astype(f16)
+    tied = lax.all_to_all(tied, "dp", 0, 0, axis_index_groups=same_core, tiled=True)
 
     half = tokens // 2
     up4, down4 = lax.ppermute(up3[:half], "vocab", z_shift(1)), lax.ppermute(down3[half:], "vocab", z_shift(-1))
-    sums = lax.all_to_all(sums, "dp", 0, 0, axis_index_groups=same_core_parity, tiled=True)
-    sums = sums.reshape(own_cols, vocab_rows)
-
     hid_sum = hid_terms(
         emb_cols, [z, z + 7, z + 1, z + 6, z + 2], [scaled, up1, down1, up2, down2]
     )
@@ -199,7 +228,7 @@
         emb_cols, [z + 5, z + 3, z + 4], [up3, down3, jnp.concatenate([up4, down4], axis=0)], hid_sum
     ).T
 
-    embed_grad = ((jnp.sum(tied.astype(f32), axis=0) + sums.astype(f32)) * (1.0 / emb_scale)).T
+    embed_grad = (jnp.sum(after(tied, hidden_grad).astype(f32), axis=0) * (1.0 / emb_scale)).T
     return (token_loss, hidden_grad, embed_grad)
 
 

time: 164 us -> 149 us (0.909)
  starting transfers between devices: 54.6 us -> 44.7 us
  Pallas kernels: 19.3 us -> 14.3 us
  local copies, waits for them, and re-layouts: 13.7 us -> 11.8 us
    ppermute x1, waiting for transfers between devices: 0.01 us -> 9.86 us  [per_device(): lax.ppermute(down2, 'vocab', z_shift(-1))]
    all_to_all x2 -> x1, waiting for transfers between devices: 13.2 us -> 4.19 us  [per_device(): lax.all_to_all(after(sums, up1, down1), 'vocab', 0, 0, tiled=True)]
    all_to_all x2 -> x1, starting transfers between devices: 11.9 us -> 4.55 us  [per_device(): lax.all_to_all(after(sums, up1, down1), 'vocab', 0, 0, tiled=True)]
    ppermute x1, waiting for transfers between devices: 9.94 us -> 3.45 us  [per_device(): lax.ppermute(down1, 'vocab', z_shift(-1))]
    pallas_call x1, Pallas kernels: 9.54 us -> 4.34 us  [segment_sum(): pl.pallas_call(segment_kernel, out_shape=jax.ShapeDtypeStruct((NZ, cols,...]
    ppermute x1, waiting for transfers between devices: 0.01 us -> 3.49 us  [per_device(): lax.ppermute(down3[half:], 'vocab', z_shift(-1))]
    ppermute x1, waiting for transfers between devices: 5.47 us -> 2.48 us  [per_device(): lax.ppermute(scaled, 'vocab', z_shift(1))]
    ppermute x1, starting transfers between devices: 3.64 us -> 0.92 us  [per_device(): lax.ppermute(down2, 'vocab', z_shift(-1))]
  transfers between devices with their start and end apart: 19 -> 18, of which waited for: 10 -> 12; matrix products, arithmetic and copies ran while one was open for 17% -> 14% of each run, Pallas kernels for 8% -> 10%
where the time goes in v2:
time: 149 us
  starting transfers between devices  44.7 us (30%)
  waiting for transfers between devices  40.6 us (27%)
  matrix products  14.7 us (10%)
  Pallas kernels  14.3 us (10%)
  between operations  14.3 us (10%)
  local copies, waits for them, and re-layouts  11.8 us (8%)
  other arithmetic  8.38 us (6%)
    ppermute x1, waiting for transfers between devices, per_device(): lax.ppermute(down2, 'vocab', z_shift(-1))  9.86 us
    unnamed x22, local copies, waits for them, and re-layouts  8.99 us
    all_to_all x1, starting transfers between devices, per_device(): emb_few = lax.all_to_all(emb_few, 'vocab', 0, 0, tiled=True)  8.47 us
    all_to_all x1, starting transfers between devices, per_device(): packed = lax.all_to_all(packed, 'dp', 0, 0, tiled=True)  7.62 us
    dot_general x1, matrix products, per_device(): jnp.einsum('td,vd->tv', hidden, embedding, preferred_element_type=f32)  7.45 us
    dot_general x1, matrix products, per_device(): jnp.einsum('kdt,tv->kdv', hid_pair, terms, preferred_element_type=f32)  7.27 us
    all_to_all x1, starting transfers between devices, per_device(): lax.all_to_all(tied, 'dp', 0, 0, axis_index_groups=same_core, tiled=True)  7.24 us
    pallas_call x2, Pallas kernels, hid_terms(): pl.pallas_call(lambda *refs: hid_kernel(len(blocks), last, *refs), out_sh...  5.88 us
  transfers between devices with their start and end apart: 18, of which 12 were waited for; matrix products, arithmetic and copies ran while one was open for 14% of the time, Pallas kernels for 10%

profile of v2, /device:TPU:2, one launch (start us, length us, event | category | flops | bytes accessed | tf_op | source)
XLA Modules:
  0.0 148.7 jit_solution(14533714647154189484)
XLA Ops:
  7.2 0.9 constant_dynamic-slice_fusion
  8.1 0.2 reshape.48
  8.3 0.7 copy.10
  8.9 8.5 %all-to-all-start.1 = ((bf16[8,16,576]{2,1,0:T(8,128)(2,1)}), bf16[8,16,576]{2,1,0:T(8,128)(2,1)S(1)}, u32[]{:S(2)}, u32[]{:S(2)}) async-start(bf16[8,16,576]{2,1,0:T(8,128)(2,1)} %copy.10), calls=%async_computation.1 | async-start | bytes 327680 | tf_op jit(solution)/shard_map/all_to_all | solution.py:172
  17.4 0.0 all-gather.3.cloned.1.call-start
  17.5 0.7 broadcast_subtract_fusion
  18.2 7.5 %exponential_reduce_fusion = (f32[512]{0:T(512)S(1)}, f32[512]{0:T(512)S(1)}, f32[512,512]{1,0:T(8,128)S(1)}) fusion(s32[512]{0:T(512)S(1)} %broadcast_subtract_fusion, bf16[512,4608]{1,0:T(8,128)(2,1)} %x_ref, bf16[512,4608]{1,0:T(8,128)(2,1)} %param.5), kind=kOutput, calls=%fused_computation.38 | convolution fusion | flops 2417490944 | bytes 10491904 | tf_op jit(solution)/shard_map/td,vd->tv/dot_general | solution.py:174
  25.6 1.6 %all-to-all-done.1 = bf16[8,16,576]{2,1,0:T(8,128)(2,1)S(1)} async-done(((bf16[8,16,576]{2,1,0:T(8,128)(2,1)}), bf16[8,16,576]{2,1,0:T(8,128)(2,1)S(1)}, u32[]{:S(2)}, u32[]{:S(2)}) %all-to-all-start.1) | async-done | bytes 147488 | tf_op jit(solution)/shard_map/all_to_all | solution.py:172
  27.2 0.7 copy-done.10
  27.8 0.0 all-gather.3.cloned.1.call-update
  27.9 1.0 shard_map.76
  28.9 7.6 %all-to-all-start = ((bf16[32,80,128]{2,1,0:T(8,128)(2,1)}), bf16[32,80,128]{2,1,0:T(8,128)(2,1)S(1)}, u32[]{:S(2)}, u32[]{:S(2)}) async-start(bf16[32,80,128]{2,1,0:T(8,128)(2,1)} %shard_map.76), calls=%async_computation | async-start | bytes 1310720 | tf_op jit(solution)/shard_map/all_to_all | solution.py:185
  36.5 0.7 collective-permute-start
  37.2 3.0 %collective-permute-done = f32[2,512]{1,0:T(2,128)S(1)} collective-permute-done((f32[2,512]{1,0:T(2,128)S(1)}, f32[2,512]{1,0:T(2,128)S(1)}, u32[]{:S(2)}, u32[]{:S(2)}) %collective-permute-start) | collective-permute-done | bytes 4128 | tf_op jit(solution)/shard_map/ppermute | solution.py:180
  40.2 1.4 collective-permute-start.1
  41.7 3.2 %collective-permute-done.1 = f32[2,512]{1,0:T(2,128)S(1)} collective-permute-done((f32[2,512]{1,0:T(2,128)S(1)}, f32[2,512]{1,0:T(2,128)S(1)}, u32[]{:S(2)}, u32[]{:S(2)}) %collective-permute-start.1) | collective-permute-done | bytes 4128 | tf_op jit(solution)/shard_map/ppermute | solution.py:184
  44.9 4.3 %collective-permute-start.2 = (f32[2,512]{1,0:T(2,128)S(1)}, f32[2,512]{1,0:T(2,128)S(1)}, u32[]{:S(2)}, u32[]{:S(2)}) collective-permute-start(f32[2,512]{1,0:T(2,128)S(1)} %add.105), channel_id=1, source_target_pairs={{0,4},{1,5},{2,6},{3,7},{4,0},{5,1},{6,2},{7,3},{8,12},{9,13},{10,... | collective-permute-start | bytes 12296 | tf_op jit(solution)/shard_map/ppermute | solution.py:187
  49.2 3.2 %collective-permute-done.2 = f32[2,512]{1,0:T(2,128)S(1)} collective-permute-done((f32[2,512]{1,0:T(2,128)S(1)}, f32[2,512]{1,0:T(2,128)S(1)}, u32[]{:S(2)}, u32[]{:S(2)}) %collective-permute-start.2) | collective-permute-done | bytes 4128 | tf_op jit(solution)/shard_map/ppermute | solution.py:187
  52.4 0.0 all-to-all-done.x_ref
  52.4 0.4 multiply_convert_fusion.1.refs_2_
  52.8 1.7 %collective-permute-start.6 = (bf16[512,512]{1,0:T(8,128)(2,1)S(1)}, bf16[512,512]{1,0:T(8,128)(2,1)S(1)}, u32[]{:S(2)}, u32[]{:S(2)}) collective-permute-start(bf16[512,512]{1,0:T(8,128)(2,1)S(1)} %multiply_convert_fusion.1.refs_2_), channel_id=1, source_target_pairs={{0,7},{1,0},{2,1},{3,2},{4,3},{5,4},{6,5},{7,6},{8,15},{9,8},{10,9... | collective-permute-start | bytes 1572872 | tf_op jit(solution)/shard_map/ppermute | solution.py:195
  54.5 0.4 collective-permute-start.3
  54.9 2.3 %copy-done.2 = bf16[512,4608]{1,0:T(8,128)(2,1)S(1)} copy-done((bf16[512,4608]{1,0:T(8,128)(2,1)S(1)}, bf16[512,4608]{1,0:T(8,128)(2,1)}, u32[]{:S(2)}) %copy-start.2) | copy-done | bytes 4718616
  57.3 3.0 %shard_map.79 = (bf16[16,144,512]{2,1,0:T(8,128)(2,1)S(1)}, bf16[16,144,512]{2,1,0:T(8,128)(2,1)}) custom-call(s32[1]{0:T(128)} %bitcast.17.core_ref, bf16[512,4608]{1,0:T(8,128)(2,1)S(1)} %copy-done.2), custom_call_target="tpu_custom_call" | custom-call | bytes 9437184 | tf_op jit(solution)/shard_map/pallas_call | solution.py:146
  60.3 1.4 copy-done.9
  61.7 0.0 collective-permute-start.11
  61.8 0.5 collective-permute-start.12
  62.3 1.7 %collective-permute-done.6.refs_4_ = bf16[512,512]{1,0:T(8,128)(2,1)S(1)} collective-permute-done((bf16[512,512]{1,0:T(8,128)(2,1)S(1)}, bf16[512,512]{1,0:T(8,128)(2,1)S(1)}, u32[]{:S(2)}, u32[]{:S(2)}) %collective-permute-start.6) | collective-permute-done | bytes 524320 | tf_op jit(solution)/shard_map/ppermute | solution.py:195
  64.1 2.5 %collective-permute-done.3.refs_3_ = bf16[512,512]{1,0:T(8,128)(2,1)S(1)} collective-permute-done((bf16[512,512]{1,0:T(8,128)(2,1)S(1)}, bf16[512,512]{1,0:T(8,128)(2,1)S(1)}, u32[]{:S(2)}, u32[]{:S(2)}) %collective-permute-start.3) | collective-permute-done | bytes 524320 | tf_op jit(solution)/shard_map/ppermute | solution.py:195
  66.6 4.3 %shard_map.80 = f32[8,18,512]{2,1,0:T(8,128)S(1)} custom-call(bf16[32,80,128]{2,1,0:T(8,128)(2,1)S(1)} %all-to-all-done.x_ref), custom_call_target="tpu_custom_call" | custom-call | flops 5000000000 | bytes 2000000 | tf_op jit(solution)/shard_map/pallas_call | solution.py:57
  71.0 0.8 reshape.49
  71.7 4.5 %all-to-all-start.2 = ((f16[8,72,128]{2,1,0:T(8,128)(2,1)}), f16[8,72,128]{2,1,0:T(8,128)(2,1)S(1)}, u32[]{:S(2)}, u32[]{:S(2)}) async-start(f16[8,72,128]{2,1,0:T(8,128)(2,1)} %reshape.49), calls=%async_computation.2 | async-start | bytes 294912 | tf_op jit(solution)/shard_map/all_to_all | solution.py:210
  76.3 3.2 %collective-permute-start.7 = (bf16[512,512]{1,0:T(8,128)(2,1)S(1)}, bf16[512,512]{1,0:T(8,128)(2,1)S(1)}, u32[]{:S(2)}, u32[]{:S(2)}) collective-permute-start(bf16[512,512]{1,0:T(8,128)(2,1)S(1)} %collective-permute-done.6.refs_4_), channel_id=1, source_target_pairs={{0,7},{1,0},{2,1},{3,2},{4,3},{5,4},{6,5},{7,6},{8,15},{9,8},{10,9... | collective-permute-start | bytes 1572872 | tf_op jit(solution)/shard_map/ppermute | solution.py:206
  79.5 0.0 collective-permute-start.4
  79.5 2.7 %select_convert_fusion = bf16[16,144,288]{2,1,0:T(8,128)(2,1)} fusion(s32[]{:T(128)S(6)} %mul.63, s32[]{:T(128)S(6)} %select_n.91, s32[288]{0:T(512)S(1)} %get-tuple-element.32, s32[288]{0:T(512)S(1)} %get-tuple-element.33, s32[16,144]{1,0:T(8,128)S(1)} %multiply_add_fusion, pred[288]{0:T(512)(128)(4,1)S(1)} %fusion.31), kind=kLoop, calls=%fused_computation.22 | loop fusion | flops 13934592 | bytes 1338920 | tf_op jit(solution)/shard_map/convert_element_type | solution.py:203
  82.2 4.2 %all-to-all-done.2 = f16[8,72,128]{2,1,0:T(8,128)(2,1)S(1)} async-done(((f16[8,72,128]{2,1,0:T(8,128)(2,1)}), f16[8,72,128]{2,1,0:T(8,128)(2,1)S(1)}, u32[]{:S(2)}, u32[]{:S(2)}) %all-to-all-start.2) | async-done | bytes 147488 | tf_op jit(solution)/shard_map/all_to_all | solution.py:210
  86.5 0.1 convert_element_type.42
  86.7 3.5 %collective-permute-done.7.refs_6_ = bf16[512,512]{1,0:T(8,128)(2,1)S(1)} collective-permute-done((bf16[512,512]{1,0:T(8,128)(2,1)S(1)}, bf16[512,512]{1,0:T(8,128)(2,1)S(1)}, u32[]{:S(2)}, u32[]{:S(2)}) %collective-permute-start.7) | collective-permute-done | bytes 524320 | tf_op jit(solution)/shard_map/ppermute | solution.py:206
  90.1 2.3 %collective-permute-done.4.refs_5_ = bf16[512,512]{1,0:T(8,128)(2,1)S(1)} collective-permute-done((bf16[512,512]{1,0:T(8,128)(2,1)S(1)}, bf16[512,512]{1,0:T(8,128)(2,1)S(1)}, u32[]{:S(2)}, u32[]{:S(2)}) %collective-permute-start.4) | collective-permute-done | bytes 524320 | tf_op jit(solution)/shard_map/ppermute | solution.py:206
  92.4 0.0 collective-permute-done.12
  92.4 0.0 collective-permute-done.11
  92.4 7.3 %multiply_convert_fusion = f16[16,144,512]{2,1,0:T(8,128)(2,1)} fusion(bf16[16,144,288]{2,1,0:T(8,128)(2,1)} %select_convert_fusion, bf16[16,144,512]{2,1,0:T(8,128)(2,1)} %collective-permute-done.11, bf16[16,144,512]{2,1,0:T(8,128)(2,1)} %copy-done.9, bf16[144,512]{1,0:T(8,128)(2,1)S(1)} %subtract_convert_fusion, ...), kind=kOutput, calls=%fused_computation.15 | convolution fusion | flops 3121266688 | bytes 9748480 | tf_op jit(solution)/shard_map/kdt,tv->kdv/dot_general | solution.py:218
  99.7 7.2 %all-to-all-start.3 = ((f16[16,144,512]{2,1,0:T(8,128)(2,1)}), f16[16,144,512]{2,1,0:T(8,128)(2,1)}, u32[]{:S(2)}, u32[]{:S(2)}) async-start(f16[16,144,512]{2,1,0:T(8,128)(2,1)} %multiply_convert_fusion), calls=%async_computation.3 | async-start | bytes 4718592 | tf_op jit(solution)/shard_map/all_to_all | solution.py:220
  106.9 0.9 collective-permute-start.8
  107.9 1.4 collective-permute-start.5
  109.2 9.9 %collective-permute-done.8.refs_3_ = bf16[512,512]{1,0:T(8,128)(2,1)S(1)} collective-permute-done((bf16[512,512]{1,0:T(8,128)(2,1)S(1)}, bf16[512,512]{1,0:T(8,128)(2,1)S(1)}, u32[]{:S(2)}, u32[]{:S(2)}) %collective-permute-start.8) | collective-permute-done | bytes 524320 | tf_op jit(solution)/shard_map/ppermute | solution.py:214
  119.1 0.7 collective-permute-start.10
  119.8 0.0 collective-permute-done.5.refs_2_
  119.9 1.4 collective-permute-start.9
  121.3 0.1 pad_add_fusion.refs_0_
  121.4 0.1 stack.51.refs_0_
  121.5 0.6 log_subtract_fusion
  122.1 3.5 %collective-permute-done.10 = bf16[256,512]{1,0:T(8,128)(2,1)S(1)} collective-permute-done((bf16[256,512]{1,0:T(8,128)(2,1)S(1)}, bf16[256,512]{1,0:T(8,128)(2,1)S(1)}, u32[]{:S(2)}, u32[]{:S(2)}) %collective-permute-start.10) | collective-permute-done | bytes 262176 | tf_op jit(solution)/shard_map/ppermute | solution.py:223
  125.6 2.1 %collective-permute-done.9 = bf16[256,512]{1,0:T(8,128)(2,1)} collective-permute-done((bf16[256,512]{1,0:T(8,128)(2,1)S(1)}, bf16[256,512]{1,0:T(8,128)(2,1)}, u32[]{:S(2)}, u32[]{:S(2)}) %collective-permute-start.9) | collective-permute-done | bytes 262176 | tf_op jit(solution)/shard_map/ppermute | solution.py:223
  127.6 1.0 pad_maximum_fusion.refs_4_
  128.6 0.0 all-gather.3.cloned.1.call-done
  128.7 2.5 %copy-done = bf16[256,16,576]{2,1,0:T(8,128)(2,1)S(1)} copy-done((bf16[256,16,576]{2,1,0:T(8,128)(2,1)S(1)}, bf16[256,16,576]{2,1,0:T(8,128)(2,1)}, u32[]{:S(2)}) %copy-start) | copy-done | bytes 4718616
  131.1 1.0 copy-done.5
  132.2 1.0 copy-done.7
  133.2 2.8 %shard_map.77.refs_5_ = f32[512,576]{1,0:T(8,128)S(1)} custom-call(s32[5]{0:T(128)S(1)} %stack.51.refs_0_, bf16[32,8,16,576]{3,2,1,0:T(8,128)(2,1)S(1)} %bitcast.25, bf16[512,512]{1,0:T(8,128)(2,1)S(1)} %multiply_convert_fusion.1.refs_2_, bf16[512,512]{1,0:T(8,128)(2,1)S(1)} %collective-permute-done.3.refs_3_, ...), custom_call_target="tpu_custom_call" | custom-call | flops 1509949440 | bytes 8388608 | tf_op jit(solution)/shard_map/pallas_call | solution.py:93
  136.0 3.1 %shard_map.78 = f32[576,512]{1,0:T(8,128)} custom-call(s32[3]{0:T(128)S(1)} %pad_add_fusion.refs_0_, bf16[32,8,16,576]{3,2,1,0:T(8,128)(2,1)S(1)} %bitcast.26, bf16[512,512]{1,0:T(8,128)(2,1)S(1)} %collective-permute-done.5.refs_2_, bf16[512,512]{1,0:T(8,128)(2,1)S(1)} %collective-permute-done.8.refs_3_, bf16[512,512]{1,0:T(8,128)(2,1)S(1)} %pad_maximum_fusion.refs_4_, ...), custom_call_target="tpu_custom_call" | custom-call | flops 905969664 | bytes 8388608 | tf_op jit(solution)/shard_map/pallas_call | solution.py:93
  139.1 0.0 all-to-all-done.3
  139.1 2.0 %convert_reduce_fusion = f32[144,512]{1,0:T(8,128)S(1)} fusion(f16[16,144,512]{2,1,0:T(8,128)(2,1)} %all-to-all-done.3), kind=kLoop, calls=%fused_computation.14 | loop fusion | flops 2285568 | bytes 2654208 | tf_op jit(solution)/shard_map/reduce_sum | solution.py:231
  141.1 0.7 multiply_bitcast_fusion
  (30 shorter events, 0.3 us)
Async XLA Ops:
  8.9 18.2 %all-to-all-start.1 = ((bf16[8,16,576]{2,1,0:T(8,128)(2,1)}), bf16[8,16,576]{2,1,0:T(8,128)(2,1)S(1)}, u32[]{:S(2)}, u32[]{:S(2)}) async-start(bf16[8,16,576]{2,1,0:T(8,128)(2,1)} %copy.10), calls=%async_computation.1 | async-start | bytes 327680 | tf_op jit(solution)/shard_map/all_to_all | solution.py:172
  17.4 111.2 %all-gather.3.cloned.1.call-start = ((), (), s32[]{:S(2)}) async-start(), calls=%async_computation.4 | async-start | bytes 5406720 | tf_op jit(solution)/shard_map/all_gather | solution.py:181
  18.1 9.7 %copy-start.3 = (bf16[512,576]{0,1:T(8,128)(2,1)S(1)}, bf16[512,576]{0,1:T(8,128)(2,1)}, u32[]{:S(2)}) copy-start(bf16[512,576]{0,1:T(8,128)(2,1)} %param.9) | copy-start | bytes 1769476
  18.1 9.7 %copy-start.8 = (s32[512]{0:T(512)S(1)}, s32[512]{0:T(512)}, u32[]{:S(2)}) copy-start(s32[512]{0:T(512)} %param.8) | copy-start | bytes 6148
  27.2 0.7 copy-start.10
  28.9 23.5 %all-to-all-start = ((bf16[32,80,128]{2,1,0:T(8,128)(2,1)}), bf16[32,80,128]{2,1,0:T(8,128)(2,1)S(1)}, u32[]{:S(2)}, u32[]{:S(2)}) async-start(bf16[32,80,128]{2,1,0:T(8,128)(2,1)} %shard_map.76), calls=%async_computation | async-start | bytes 1310720 | tf_op jit(solution)/shard_map/all_to_all | solution.py:185
  36.5 3.7 %collective-permute-start = (f32[2,512]{1,0:T(2,128)S(1)}, f32[2,512]{1,0:T(2,128)S(1)}, u32[]{:S(2)}, u32[]{:S(2)}) collective-permute-start(f32[2,512]{1,0:T(2,128)S(1)} %pad_maximum_fusion.1), channel_id=1, source_target_pairs={{0,1},{1,0},{2,3},{3,2},{4,5},{5,4},{6,7},{7,6},{8,9},{9,8},{10,11... | collective-permute-start | bytes 12296 | tf_op jit(solution)/shard_map/ppermute | solution.py:180
  40.2 4.6 %collective-permute-start.1 = (f32[2,512]{1,0:T(2,128)S(1)}, f32[2,512]{1,0:T(2,128)S(1)}, u32[]{:S(2)}, u32[]{:S(2)}) collective-permute-start(f32[2,512]{1,0:T(2,128)S(1)} %fusion.33), channel_id=1, source_target_pairs={{0,2},{1,3},{2,0},{3,1},{4,6},{5,7},{6,4},{7,5},{8,10},{9,11},{10,... | collective-permute-start | bytes 12296 | tf_op jit(solution)/shard_map/ppermute | solution.py:184
  44.9 7.5 %collective-permute-start.2 = (f32[2,512]{1,0:T(2,128)S(1)}, f32[2,512]{1,0:T(2,128)S(1)}, u32[]{:S(2)}, u32[]{:S(2)}) collective-permute-start(f32[2,512]{1,0:T(2,128)S(1)} %add.105), channel_id=1, source_target_pairs={{0,4},{1,5},{2,6},{3,7},{4,0},{5,1},{6,2},{7,3},{8,12},{9,13},{10,... | collective-permute-start | bytes 12296 | tf_op jit(solution)/shard_map/ppermute | solution.py:187
  52.8 11.2 %collective-permute-start.6 = (bf16[512,512]{1,0:T(8,128)(2,1)S(1)}, bf16[512,512]{1,0:T(8,128)(2,1)S(1)}, u32[]{:S(2)}, u32[]{:S(2)}) collective-permute-start(bf16[512,512]{1,0:T(8,128)(2,1)S(1)} %multiply_convert_fusion.1.refs_2_), channel_id=1, source_target_pairs={{0,7},{1,0},{2,1},{3,2},{4,3},{5,4},{6,5},{7,6},{8,15},{9,8},{10,9... | collective-permute-start | bytes 1572872 | tf_op jit(solution)/shard_map/ppermute | solution.py:195
  54.5 12.0 %collective-permute-start.3 = (bf16[512,512]{1,0:T(8,128)(2,1)S(1)}, bf16[512,512]{1,0:T(8,128)(2,1)S(1)}, u32[]{:S(2)}, u32[]{:S(2)}) collective-permute-start(bf16[512,512]{1,0:T(8,128)(2,1)S(1)} %multiply_convert_fusion.1.refs_2_), channel_id=1, source_target_pairs={{0,1},{1,2},{2,3},{3,4},{4,5},{5,6},{6,7},{7,0},{8,9},{9,10},{10,1... | collective-permute-start | bytes 1572872 | tf_op jit(solution)/shard_map/ppermute | solution.py:195
  54.9 2.3 %copy-start.2 = (bf16[512,4608]{1,0:T(8,128)(2,1)S(1)}, bf16[512,4608]{1,0:T(8,128)(2,1)}, u32[]{:S(2)}) copy-start(bf16[512,4608]{1,0:T(8,128)(2,1)} %x_ref) | copy-start | bytes 14155780
  60.3 1.4 copy-start.9
  61.7 30.7 %collective-permute-start.11 = (bf16[16,144,512]{2,1,0:T(8,128)(2,1)}, bf16[16,144,512]{2,1,0:T(8,128)(2,1)}, u32[]{:S(2)}, u32[]{:S(2)}) collective-permute-start(bf16[16,144,512]{2,1,0:T(8,128)(2,1)} %get-tuple-element.20), channel_id=1, source_target_pairs={{0,8},{8,0},{16,24},{24,16},{32,40},{40,32},{48,56},{56,48},{64,72... | collective-permute-start | bytes 7077896 | tf_op jit(solution)/shard_map/ppermute | solution.py:199
  61.8 30.6 %collective-permute-start.12 = (bf16[512,512]{1,0:T(8,128)(2,1)S(1)}, bf16[512,512]{1,0:T(8,128)(2,1)}, u32[]{:S(2)}, u32[]{:S(2)}) collective-permute-start(bf16[512,512]{1,0:T(8,128)(2,1)S(1)} %multiply_convert_fusion.1.refs_2_), channel_id=1, source_target_pairs={{0,8},{8,0},{16,24},{24,16},{32,40},{40,32},{48,56},{56,48},{64,72... | collective-permute-start | bytes 1572872 | tf_op jit(solution)/shard_map/ppermute | solution.py:196
  71.7 14.7 %all-to-all-start.2 = ((f16[8,72,128]{2,1,0:T(8,128)(2,1)}), f16[8,72,128]{2,1,0:T(8,128)(2,1)S(1)}, u32[]{:S(2)}, u32[]{:S(2)}) async-start(f16[8,72,128]{2,1,0:T(8,128)(2,1)} %reshape.49), calls=%async_computation.2 | async-start | bytes 294912 | tf_op jit(solution)/shard_map/all_to_all | solution.py:210
  76.3 13.8 %collective-permute-start.7 = (bf16[512,512]{1,0:T(8,128)(2,1)S(1)}, bf16[512,512]{1,0:T(8,128)(2,1)S(1)}, u32[]{:S(2)}, u32[]{:S(2)}) collective-permute-start(bf16[512,512]{1,0:T(8,128)(2,1)S(1)} %collective-permute-done.6.refs_4_), channel_id=1, source_target_pairs={{0,7},{1,0},{2,1},{3,2},{4,3},{5,4},{6,5},{7,6},{8,15},{9,8},{10,9... | collective-permute-start | bytes 1572872 | tf_op jit(solution)/shard_map/ppermute | solution.py:206
  79.5 12.9 %collective-permute-start.4 = (bf16[512,512]{1,0:T(8,128)(2,1)S(1)}, bf16[512,512]{1,0:T(8,128)(2,1)S(1)}, u32[]{:S(2)}, u32[]{:S(2)}) collective-permute-start(bf16[512,512]{1,0:T(8,128)(2,1)S(1)} %collective-permute-done.3.refs_3_), channel_id=1, source_target_pairs={{0,1},{1,2},{2,3},{3,4},{4,5},{5,6},{6,7},{7,0},{8,9},{9,10},{10,1... | collective-permute-start | bytes 1572872 | tf_op jit(solution)/shard_map/ppermute | solution.py:206
  90.1 16.8 %copy-start.4 = (bf16[512,512]{1,0:T(8,128)(2,1)}, bf16[512,512]{1,0:T(8,128)(2,1)S(1)}, u32[]{:S(2)}) copy-start(bf16[512,512]{1,0:T(8,128)(2,1)S(1)} %collective-permute-done.7.refs_6_) | copy-start | bytes 1572868
  92.4 7.3 %copy-start.6 = (bf16[512,512]{1,0:T(8,128)(2,1)}, bf16[512,512]{1,0:T(8,128)(2,1)S(1)}, u32[]{:S(2)}) copy-start(bf16[512,512]{1,0:T(8,128)(2,1)S(1)} %collective-permute-done.4.refs_5_) | copy-start | bytes 1572868
  99.7 39.4 %all-to-all-start.3 = ((f16[16,144,512]{2,1,0:T(8,128)(2,1)}), f16[16,144,512]{2,1,0:T(8,128)(2,1)}, u32[]{:S(2)}, u32[]{:S(2)}) async-start(f16[16,144,512]{2,1,0:T(8,128)(2,1)} %multiply_convert_fusion), calls=%async_computation.3 | async-start | bytes 4718592 | tf_op jit(solution)/shard_map/all_to_all | solution.py:220
  106.9 12.1 %collective-permute-start.8 = (bf16[512,512]{1,0:T(8,128)(2,1)S(1)}, bf16[512,512]{1,0:T(8,128)(2,1)S(1)}, u32[]{:S(2)}, u32[]{:S(2)}) collective-permute-start(bf16[512,512]{1,0:T(8,128)(2,1)S(1)} %collective-permute-done.7.refs_6_), channel_id=1, source_target_pairs={{0,7},{1,0},{2,1},{3,2},{4,3},{5,4},{6,5},{7,6},{8,15},{9,8},{10,9... | collective-permute-start | bytes 1572872 | tf_op jit(solution)/shard_map/ppermute | solution.py:214
  107.9 12.0 %collective-permute-start.5 = (bf16[512,512]{1,0:T(8,128)(2,1)}, bf16[512,512]{1,0:T(8,128)(2,1)S(1)}, u32[]{:S(2)}, u32[]{:S(2)}) collective-permute-start(bf16[512,512]{1,0:T(8,128)(2,1)} %copy-done.6), channel_id=1, source_target_pairs={{0,1},{1,2},{2,3},{3,4},{4,5},{5,6},{6,7},{7,0},{8,9},{9,10},{10,1... | collective-permute-start | bytes 1572872 | tf_op jit(solution)/shard_map/ppermute | solution.py:214
  119.1 6.5 %collective-permute-start.10 = (bf16[256,512]{1,0:T(8,128)(2,1)S(1)}, bf16[256,512]{1,0:T(8,128)(2,1)S(1)}, u32[]{:S(2)}, u32[]{:S(2)}) collective-permute-start(bf16[256,512]{1,0:T(8,128)(2,1)S(1)} %slice.17), channel_id=1, source_target_pairs={{0,7},{1,0},{2,1},{3,2},{4,3},{5,4},{6,5},{7,6},{8,15},{9,8},{10,9... | collective-permute-start | bytes 786440 | tf_op jit(solution)/shard_map/ppermute | solution.py:223
  119.9 7.8 %collective-permute-start.9 = (bf16[256,512]{1,0:T(8,128)(2,1)S(1)}, bf16[256,512]{1,0:T(8,128)(2,1)}, u32[]{:S(2)}, u32[]{:S(2)}) collective-permute-start(bf16[256,512]{1,0:T(8,128)(2,1)S(1)} %slice.16), channel_id=1, source_target_pairs={{0,1},{1,2},{2,3},{3,4},{4,5},{5,6},{6,7},{7,0},{8,9},{9,10},{10,1... | collective-permute-start | bytes 786440 | tf_op jit(solution)/shard_map/ppermute | solution.py:223
  128.7 2.5 %copy-start = (bf16[256,16,576]{2,1,0:T(8,128)(2,1)S(1)}, bf16[256,16,576]{2,1,0:T(8,128)(2,1)}, u32[]{:S(2)}) copy-start(bf16[256,16,576]{2,1,0:T(8,128)(2,1)} %all-gather.3.cloned.1.call-done) | copy-start | bytes 14155780
  131.1 1.0 copy-start.5
  132.2 1.0 copy-start.7
  133.2 2.8 %copy-start.1 = (bf16[256,16,576]{2,1,0:T(8,128)(2,1)S(1)}, bf16[256,16,576]{2,1,0:T(8,128)(2,1)}, u32[]{:S(2)}) copy-start(bf16[256,16,576]{2,1,0:T(8,128)(2,1)} %all-gather.3.cloned.1.call-done) | copy-start | bytes 14155780
Sparse Core Ops, SparseCore 0:
  28.0 53.6 all-gather.2

commit v3 on v2

--- a/solution.py
+++ b/solution.py
@@ -205,25 +205,25 @@
 
     up2, down2 = lax.ppermute(up1, "vocab", z_shift(1)), lax.ppermute(down1, "vocab", z_shift(-1))
 
-    sums = segment_sum(after(packed, up1, down1))
+    sums = segment_sum(after(packed, hid_own, scaled))
     sums = (sums * emb_scale).astype(f16).reshape(NZ, cols * vocab_rows // 128, 128)
     sums = lax.all_to_all(after(sums, up1, down1), "vocab", 0, 0, tiled=True).reshape(NZ * cols, vocab_rows)
     sums_high = sums.astype(bf16)
     sums_low = (sums.astype(f32) - sums_high.astype(f32)).astype(bf16)
 
-    up3, down3 = lax.ppermute(up2, "vocab", z_shift(1)), lax.ppermute(down2, "vocab", z_shift(-1))
-
-    sums_high = after(sums_high, up2, down2)
-    terms = jnp.concatenate([scaled, scaled_other, sums_high, sums_low])
-    tied = jnp.einsum("kdt,tv->kdv", hid_pair, terms, preferred_element_type=f32)
-    tied = (tied * emb_scale).astype(f16)
-    tied = lax.all_to_all(tied, "dp", 0, 0, axis_index_groups=same_core, tiled=True)
-
-    half = tokens // 2
-    up4, down4 = lax.ppermute(up3[:half], "vocab", z_shift(1)), lax.ppermute(down3[half:], "vocab", z_shift(-1))
     hid_sum = hid_terms(
         emb_cols, [z, z + 7, z + 1, z + 6, z + 2], [scaled, up1, down1, up2, down2]
     )
+    up3 = lax.ppermute(up2, "vocab", z_shift(1))
+    down3 = lax.ppermute(after(down2, hid_sum), "vocab", z_shift(-1))
+
+    terms = jnp.concatenate([scaled, scaled_other, sums_high, sums_low])
+    tied = jnp.einsum("kdt,tv->kdv", hid_pair, terms, preferred_element_type=f32)
+    tied = after((tied * emb_scale).astype(f16), up2, down2)
+    tied = lax.all_to_all(tied, "dp", 0, 0, axis_index_groups=same_core, tiled=True)
+
+    half = tokens // 2
+    up4, down4 = lax.ppermute(up3[:half], "vocab", z_shift(1)), lax.ppermute(down3[half:], "vocab", z_shift(-1))
     hidden_grad = hid_terms(
         emb_cols, [z + 5, z + 3, z + 4], [up3, down3, jnp.concatenate([up4, down4], axis=0)], hid_sum
     ).T

time: 149 us -> 146 us (0.980)
  waiting for transfers between devices: 40.6 us -> 32.7 us
  starting transfers between devices: 44.7 us -> 47.8 us
  local copies, waits for them, and re-layouts: 11.8 us -> 14.3 us
    ppermute x1, waiting for transfers between devices: 2.48 us -> 7.14 us  [per_device(): lax.ppermute(scaled, 'vocab', z_shift(1))]
    ppermute x1, waiting for transfers between devices: 3.45 us -> 0.01 us  [per_device(): lax.ppermute(down1, 'vocab', z_shift(-1))]
    ppermute x1, waiting for transfers between devices: 3.19 us -> 0.01 us  [per_device(): stats3 = stats2 + lax.ppermute(stats2, 'vocab', z_xor(4))]
    ppermute x1, starting transfers between devices: 0.74 us -> 3.77 us  [per_device(): lax.ppermute(down3[half:], 'vocab', z_shift(-1))]
    unnamed x22, local copies, waits for them, and re-layouts: 8.99 us -> 11.5 us
    ppermute x1, waiting for transfers between devices: 2.08 us -> 0.01 us  [per_device(): lax.ppermute(up3[:half], 'vocab', z_shift(1))]
    ppermute x1, starting transfers between devices: 3.23 us -> 1.23 us  [per_device(): lax.ppermute(down1, 'vocab', z_shift(-1))]
    ppermute x1, starting transfers between devices: 0.01 us -> 2.01 us  [per_device(): lax.ppermute(up1, 'vocab', z_shift(1))]
  transfers between devices with their start and end apart: 18 -> 18, of which waited for: 12 -> 9; matrix products, arithmetic and copies ran while one was open for 14% -> 14% of each run, Pallas kernels for 10% -> 10%
where the time goes in v3:
time: 146 us; the launch traced here: 145 us
  starting transfers between devices  47.8 us (33%)
  waiting for transfers between devices  32.7 us (22%)
  matrix products  14.5 us (10%)
  local copies, waits for them, and re-layouts  14.3 us (10%)
  Pallas kernels  14.3 us (10%)
  between operations  14.2 us (10%)
  other arithmetic  7.44 us (5%)
    unnamed x22, local copies, waits for them, and re-layouts  11.5 us
    all_to_all x1, starting transfers between devices, per_device(): emb_few = lax.all_to_all(emb_few, 'vocab', 0, 0, tiled=True)  8.47 us
    all_to_all x1, starting transfers between devices, per_device(): packed = lax.all_to_all(packed, 'dp', 0, 0, tiled=True)  7.62 us
    dot_general x1, matrix products, per_device(): jnp.einsum('td,vd->tv', hidden, embedding, preferred_element_type=f32)  7.45 us
    all_to_all x1, starting transfers between devices, per_device(): lax.all_to_all(tied, 'dp', 0, 0, axis_index_groups=same_core, tiled=True)  7.18 us
    ppermute x1, waiting for transfers between devices, per_device(): lax.ppermute(scaled, 'vocab', z_shift(1))  7.14 us
    dot_general x1, matrix products, per_device(): jnp.einsum('kdt,tv->kdv', hid_pair, terms, preferred_element_type=f32)  7.09 us
    ppermute x1, waiting for transfers between devices, per_device(): down3 = lax.ppermute(after(down2, hid_sum), 'vocab', z_shift(-1))  6.58 us
  transfers between devices with their start and end apart: 18, of which 9 were waited for; matrix products, arithmetic and copies ran while one was open for 14% of the time, Pallas kernels for 10%

profile of v3, /device:TPU:2, one launch (start us, length us, event | category | flops | bytes accessed | tf_op | source)
XLA Modules:
  0.0 145.3 jit_solution(13606861994362641533)
XLA Ops:
  7.2 0.9 constant_dynamic-slice_fusion
  8.1 0.2 reshape.48
  8.3 0.7 copy.10
  8.9 8.5 %all-to-all-start.1 = ((bf16[8,16,576]{2,1,0:T(8,128)(2,1)}), bf16[8,16,576]{2,1,0:T(8,128)(2,1)S(1)}, u32[]{:S(2)}, u32[]{:S(2)}) async-start(bf16[8,16,576]{2,1,0:T(8,128)(2,1)} %copy.10), calls=%async_computation.1 | async-start | bytes 327680 | tf_op jit(solution)/shard_map/all_to_all | solution.py:172
  17.4 0.0 all-gather.3.cloned.1.call-start
  17.5 0.7 broadcast_subtract_fusion
  18.2 7.5 %exponential_reduce_fusion = (f32[512]{0:T(512)S(1)}, f32[512]{0:T(512)S(1)}, f32[512,512]{1,0:T(8,128)S(1)}) fusion(s32[512]{0:T(512)S(1)} %broadcast_subtract_fusion, bf16[512,4608]{1,0:T(8,128)(2,1)} %x_ref, bf16[512,4608]{1,0:T(8,128)(2,1)} %param.5), kind=kOutput, calls=%fused_computation.38 | convolution fusion | flops 2417490944 | bytes 10491904 | tf_op jit(solution)/shard_map/td,vd->tv/dot_general | solution.py:174
  25.6 1.6 %all-to-all-done.1 = bf16[8,16,576]{2,1,0:T(8,128)(2,1)S(1)} async-done(((bf16[8,16,576]{2,1,0:T(8,128)(2,1)}), bf16[8,16,576]{2,1,0:T(8,128)(2,1)S(1)}, u32[]{:S(2)}, u32[]{:S(2)}) %all-to-all-start.1) | async-done | bytes 147488 | tf_op jit(solution)/shard_map/all_to_all | solution.py:172
  27.2 0.7 copy-done.10
  27.8 0.0 all-gather.3.cloned.1.call-update
  27.9 0.0 copy-done.3
  27.9 1.0 shard_map.76
  28.9 7.6 %all-to-all-start = ((bf16[32,80,128]{2,1,0:T(8,128)(2,1)}), bf16[32,80,128]{2,1,0:T(8,128)(2,1)S(1)}, u32[]{:S(2)}, u32[]{:S(2)}) async-start(bf16[32,80,128]{2,1,0:T(8,128)(2,1)} %shard_map.76), calls=%async_computation | async-start | bytes 1310720 | tf_op jit(solution)/shard_map/all_to_all | solution.py:185
  36.5 0.7 collective-permute-start
  37.2 3.0 %collective-permute-done = f32[2,512]{1,0:T(2,128)S(1)} collective-permute-done((f32[2,512]{1,0:T(2,128)S(1)}, f32[2,512]{1,0:T(2,128)S(1)}, u32[]{:S(2)}, u32[]{:S(2)}) %collective-permute-start) | collective-permute-done | bytes 4128 | tf_op jit(solution)/shard_map/ppermute | solution.py:180
  40.2 1.4 collective-permute-start.1
  41.7 3.2 %collective-permute-done.1 = f32[2,512]{1,0:T(2,128)S(1)} collective-permute-done((f32[2,512]{1,0:T(2,128)S(1)}, f32[2,512]{1,0:T(2,128)S(1)}, u32[]{:S(2)}, u32[]{:S(2)}) %collective-permute-start.1) | collective-permute-done | bytes 4128 | tf_op jit(solution)/shard_map/ppermute | solution.py:184
  44.9 4.3 %collective-permute-start.2 = (f32[2,512]{1,0:T(2,128)S(1)}, f32[2,512]{1,0:T(2,128)S(1)}, u32[]{:S(2)}, u32[]{:S(2)}) collective-permute-start(f32[2,512]{1,0:T(2,128)S(1)} %add.105), channel_id=1, source_target_pairs={{0,4},{1,5},{2,6},{3,7},{4,0},{5,1},{6,2},{7,3},{8,12},{9,13},{10,... | collective-permute-start | bytes 12296 | tf_op jit(solution)/shard_map/ppermute | solution.py:187
  49.2 2.4 %copy-done.2 = bf16[512,4608]{1,0:T(8,128)(2,1)S(1)} copy-done((bf16[512,4608]{1,0:T(8,128)(2,1)S(1)}, bf16[512,4608]{1,0:T(8,128)(2,1)}, u32[]{:S(2)}) %copy-start.2) | copy-done | bytes 4718616
  51.6 3.0 %shard_map.79 = (bf16[16,144,512]{2,1,0:T(8,128)(2,1)S(1)}, bf16[16,144,512]{2,1,0:T(8,128)(2,1)}) custom-call(s32[1]{0:T(128)} %bitcast.17.core_ref, bf16[512,4608]{1,0:T(8,128)(2,1)S(1)} %copy-done.2), custom_call_target="tpu_custom_call" | custom-call | bytes 9437184 | tf_op jit(solution)/shard_map/pallas_call | solution.py:146
  54.6 1.4 copy-done.9
  56.0 0.0 collective-permute-start.11
  56.0 0.0 collective-permute-done.2
  56.0 0.0 all-to-all-done.x_ref
  56.0 0.4 multiply_convert_fusion.1.refs_2_
  56.5 0.6 collective-permute-start.3
  57.0 2.7 %collective-permute-start.6 = (bf16[512,512]{1,0:T(8,128)(2,1)S(1)}, bf16[512,512]{1,0:T(8,128)(2,1)S(1)}, u32[]{:S(2)}, u32[]{:S(2)}) collective-permute-start(bf16[512,512]{1,0:T(8,128)(2,1)S(1)} %multiply_convert_fusion.1.refs_2_), channel_id=1, source_target_pairs={{0,7},{1,0},{2,1},{3,2},{4,3},{5,4},{6,5},{7,6},{8,15},{9,8},{10,9... | collective-permute-start | bytes 1572872 | tf_op jit(solution)/shard_map/ppermute | solution.py:195
  59.8 0.0 collective-permute-start.12
  59.8 4.3 %shard_map.80 = f32[8,18,512]{2,1,0:T(8,128)S(1)} custom-call(bf16[32,80,128]{2,1,0:T(8,128)(2,1)S(1)} %all-to-all-done.x_ref), custom_call_target="tpu_custom_call" | custom-call | flops 5000000000 | bytes 2000000 | tf_op jit(solution)/shard_map/pallas_call | solution.py:57
  64.2 0.8 reshape.49
  64.9 7.1 %collective-permute-done.3.refs_3_ = bf16[512,512]{1,0:T(8,128)(2,1)S(1)} collective-permute-done((bf16[512,512]{1,0:T(8,128)(2,1)S(1)}, bf16[512,512]{1,0:T(8,128)(2,1)S(1)}, u32[]{:S(2)}, u32[]{:S(2)}) %collective-permute-start.3) | collective-permute-done | bytes 524320 | tf_op jit(solution)/shard_map/ppermute | solution.py:195
  72.1 0.0 collective-permute-done.6.refs_4_
  72.1 4.2 %all-to-all-start.2 = ((f16[8,72,128]{2,1,0:T(8,128)(2,1)}), f16[8,72,128]{2,1,0:T(8,128)(2,1)S(1)}, u32[]{:S(2)}, u32[]{:S(2)}) async-start(f16[8,72,128]{2,1,0:T(8,128)(2,1)} %reshape.49), calls=%async_computation.2 | async-start | bytes 294912 | tf_op jit(solution)/shard_map/all_to_all | solution.py:210
  76.3 2.7 %select_convert_fusion = bf16[16,144,288]{2,1,0:T(8,128)(2,1)} fusion(s32[]{:T(128)S(6)} %mul.63, s32[]{:T(128)S(6)} %select_n.91, s32[288]{0:T(512)S(1)} %get-tuple-element.34, s32[288]{0:T(512)S(1)} %get-tuple-element.35, s32[16,144]{1,0:T(8,128)S(1)} %multiply_add_fusion, pred[288]{0:T(512)(128)(4,1)S(1)} %fusion.31), kind=kLoop, calls=%fused_computation.22 | loop fusion | flops 13934592 | bytes 1338920 | tf_op jit(solution)/shard_map/convert_element_type | solution.py:203
  79.1 2.0 %collective-permute-start.4 = (bf16[512,512]{1,0:T(8,128)(2,1)S(1)}, bf16[512,512]{1,0:T(8,128)(2,1)S(1)}, u32[]{:S(2)}, u32[]{:S(2)}) collective-permute-start(bf16[512,512]{1,0:T(8,128)(2,1)S(1)} %collective-permute-done.3.refs_3_), channel_id=1, source_target_pairs={{0,1},{1,2},{2,3},{3,4},{4,5},{5,6},{6,7},{7,0},{8,9},{9,10},{10,1... | collective-permute-start | bytes 1572872 | tf_op jit(solution)/shard_map/ppermute | solution.py:206
  81.1 1.2 collective-permute-start.7
  82.3 3.5 %all-to-all-done.2 = f16[8,72,128]{2,1,0:T(8,128)(2,1)S(1)} async-done(((f16[8,72,128]{2,1,0:T(8,128)(2,1)}), f16[8,72,128]{2,1,0:T(8,128)(2,1)S(1)}, u32[]{:S(2)}, u32[]{:S(2)}) %all-to-all-start.2) | async-done | bytes 147488 | tf_op jit(solution)/shard_map/all_to_all | solution.py:210
  85.9 0.1 convert_element_type.42
  86.0 0.0 collective-permute-done.12
  86.0 0.0 collective-permute-done.11
  86.0 7.1 %multiply_convert_fusion = f16[16,144,512]{2,1,0:T(8,128)(2,1)} fusion(bf16[16,144,288]{2,1,0:T(8,128)(2,1)} %select_convert_fusion, bf16[16,144,512]{2,1,0:T(8,128)(2,1)} %collective-permute-done.11, bf16[16,144,512]{2,1,0:T(8,128)(2,1)} %copy-done.9, bf16[144,512]{1,0:T(8,128)(2,1)S(1)} %subtract_convert_fusion, ...), kind=kOutput, calls=%fused_computation.15 | convolution fusion | flops 3121266688 | bytes 9748480 | tf_op jit(solution)/shard_map/kdt,tv->kdv/dot_general | solution.py:221
  93.1 1.4 collective-permute-done.4.refs_5_
  94.5 0.0 collective-permute-done.7.refs_6_
  94.5 7.2 %all-to-all-start.3 = ((f16[16,144,512]{2,1,0:T(8,128)(2,1)}), f16[16,144,512]{2,1,0:T(8,128)(2,1)}, u32[]{:S(2)}, u32[]{:S(2)}) async-start(f16[16,144,512]{2,1,0:T(8,128)(2,1)} %multiply_convert_fusion), calls=%async_computation.3 | async-start | bytes 4718592 | tf_op jit(solution)/shard_map/all_to_all | solution.py:223
  101.7 0.1 stack.51.refs_0_
  101.8 1.4 collective-permute-start.5
  103.2 2.5 %copy-done = bf16[256,16,576]{2,1,0:T(8,128)(2,1)S(1)} copy-done((bf16[256,16,576]{2,1,0:T(8,128)(2,1)S(1)}, bf16[256,16,576]{2,1,0:T(8,128)(2,1)}, u32[]{:S(2)}) %copy-start) | copy-done | bytes 4718616
  105.7 1.0 copy-done.5
  106.7 1.0 copy-done.7
  107.7 2.8 %shard_map.77.refs_5_ = f32[512,576]{1,0:T(8,128)S(1)} custom-call(s32[5]{0:T(128)S(1)} %stack.51.refs_0_, bf16[32,8,16,576]{3,2,1,0:T(8,128)(2,1)S(1)} %bitcast.25, bf16[512,512]{1,0:T(8,128)(2,1)S(1)} %multiply_convert_fusion.1.refs_2_, bf16[512,512]{1,0:T(8,128)(2,1)S(1)} %copy-done.5, bf16[512,512]{1,0:T(8,128)(2,1)S(1)} %copy-done.7, ...), custom_call_target="tpu_custom_call" | custom-call | flops 1509949440 | bytes 8388608 | tf_op jit(solution)/shard_map/pallas_call | solution.py:93
  110.5 2.1 %collective-permute-start.8 = (bf16[512,512]{1,0:T(8,128)(2,1)S(1)}, bf16[512,512]{1,0:T(8,128)(2,1)S(1)}, u32[]{:S(2)}, u32[]{:S(2)}) collective-permute-start(bf16[512,512]{1,0:T(8,128)(2,1)S(1)} %collective-permute-done.7.refs_6_), channel_id=1, source_target_pairs={{0,7},{1,0},{2,1},{3,2},{4,3},{5,4},{6,5},{7,6},{8,15},{9,8},{10,9... | collective-permute-start | bytes 1572872 | tf_op jit(solution)/shard_map/ppermute | solution.py:218
  112.6 3.0 %collective-permute-done.5.refs_2_ = bf16[512,512]{1,0:T(8,128)(2,1)S(1)} collective-permute-done((bf16[512,512]{1,0:T(8,128)(2,1)S(1)}, bf16[512,512]{1,0:T(8,128)(2,1)S(1)}, u32[]{:S(2)}, u32[]{:S(2)}) %collective-permute-start.5) | collective-permute-done | bytes 524320 | tf_op jit(solution)/shard_map/ppermute | solution.py:217
  115.7 0.1 collective-permute-start.9
  115.8 6.6 %collective-permute-done.8.refs_3_ = bf16[512,512]{1,0:T(8,128)(2,1)S(1)} collective-permute-done((bf16[512,512]{1,0:T(8,128)(2,1)S(1)}, bf16[512,512]{1,0:T(8,128)(2,1)S(1)}, u32[]{:S(2)}, u32[]{:S(2)}) %collective-permute-start.8) | collective-permute-done | bytes 524320 | tf_op jit(solution)/shard_map/ppermute | solution.py:218
  122.4 3.8 %collective-permute-start.10 = (bf16[256,512]{1,0:T(8,128)(2,1)S(1)}, bf16[256,512]{1,0:T(8,128)(2,1)S(1)}, u32[]{:S(2)}, u32[]{:S(2)}) collective-permute-start(bf16[256,512]{1,0:T(8,128)(2,1)S(1)} %slice.17), channel_id=1, source_target_pairs={{0,7},{1,0},{2,1},{3,2},{4,3},{5,4},{6,5},{7,6},{8,15},{9,8},{10,9... | collective-permute-start | bytes 786440 | tf_op jit(solution)/shard_map/ppermute | solution.py:226
  126.2 0.1 pad_add_fusion.refs_0_
  126.2 0.6 log_subtract_fusion
  126.8 0.0 collective-permute-done.9
  126.8 3.2 %collective-permute-done.10 = bf16[256,512]{1,0:T(8,128)(2,1)S(1)} collective-permute-done((bf16[256,512]{1,0:T(8,128)(2,1)S(1)}, bf16[256,512]{1,0:T(8,128)(2,1)S(1)}, u32[]{:S(2)}, u32[]{:S(2)}) %collective-permute-start.10) | collective-permute-done | bytes 262176 | tf_op jit(solution)/shard_map/ppermute | solution.py:226
  130.1 2.5 %copy-done.1 = bf16[256,16,576]{2,1,0:T(8,128)(2,1)S(1)} copy-done((bf16[256,16,576]{2,1,0:T(8,128)(2,1)S(1)}, bf16[256,16,576]{2,1,0:T(8,128)(2,1)}, u32[]{:S(2)}) %copy-start.1) | copy-done | bytes 4718616
  132.6 3.1 %shard_map.78 = f32[576,512]{1,0:T(8,128)} custom-call(s32[3]{0:T(128)S(1)} %pad_add_fusion.refs_0_, bf16[32,8,16,576]{3,2,1,0:T(8,128)(2,1)S(1)} %bitcast.26, bf16[512,512]{1,0:T(8,128)(2,1)S(1)} %collective-permute-done.5.refs_2_, bf16[512,512]{1,0:T(8,128)(2,1)S(1)} %collective-permute-done.8.refs_3_, bf16[512,512]{1,0:T(8,128)(2,1)S(1)} %pad_maximum_fusion.refs_4_, ...), custom_call_target="tpu_custom_call" | custom-call | flops 905969664 | bytes 8388608 | tf_op jit(solution)/shard_map/pallas_call | solution.py:93
  135.7 0.0 all-to-all-done.3
  135.7 2.0 %convert_reduce_fusion = f32[144,512]{1,0:T(8,128)S(1)} fusion(f16[16,144,512]{2,1,0:T(8,128)(2,1)} %all-to-all-done.3), kind=kLoop, calls=%fused_computation.14 | loop fusion | flops 2285568 | bytes 2654208 | tf_op jit(solution)/shard_map/reduce_sum | solution.py:231
  137.7 0.7 multiply_bitcast_fusion
  (30 shorter events, 0.3 us)
Async XLA Ops:
  8.9 18.2 %all-to-all-start.1 = ((bf16[8,16,576]{2,1,0:T(8,128)(2,1)}), bf16[8,16,576]{2,1,0:T(8,128)(2,1)S(1)}, u32[]{:S(2)}, u32[]{:S(2)}) async-start(bf16[8,16,576]{2,1,0:T(8,128)(2,1)} %copy.10), calls=%async_computation.1 | async-start | bytes 327680 | tf_op jit(solution)/shard_map/all_to_all | solution.py:172
  17.4 85.8 %all-gather.3.cloned.1.call-start = ((), (), s32[]{:S(2)}) async-start(), calls=%async_computation.4 | async-start | bytes 5406720 | tf_op jit(solution)/shard_map/all_gather | solution.py:181
  18.1 9.7 %copy-start.3 = (bf16[512,576]{0,1:T(8,128)(2,1)S(1)}, bf16[512,576]{0,1:T(8,128)(2,1)}, u32[]{:S(2)}) copy-start(bf16[512,576]{0,1:T(8,128)(2,1)} %param.9) | copy-start | bytes 1769476
  18.1 9.7 %copy-start.8 = (s32[512]{0:T(512)S(1)}, s32[512]{0:T(512)}, u32[]{:S(2)}) copy-start(s32[512]{0:T(512)} %param.8) | copy-start | bytes 6148
  27.2 0.7 copy-start.10
  28.9 27.1 %all-to-all-start = ((bf16[32,80,128]{2,1,0:T(8,128)(2,1)}), bf16[32,80,128]{2,1,0:T(8,128)(2,1)S(1)}, u32[]{:S(2)}, u32[]{:S(2)}) async-start(bf16[32,80,128]{2,1,0:T(8,128)(2,1)} %shard_map.76), calls=%async_computation | async-start | bytes 1310720 | tf_op jit(solution)/shard_map/all_to_all | solution.py:185
  36.5 3.7 %collective-permute-start = (f32[2,512]{1,0:T(2,128)S(1)}, f32[2,512]{1,0:T(2,128)S(1)}, u32[]{:S(2)}, u32[]{:S(2)}) collective-permute-start(f32[2,512]{1,0:T(2,128)S(1)} %pad_maximum_fusion.1), channel_id=1, source_target_pairs={{0,1},{1,0},{2,3},{3,2},{4,5},{5,4},{6,7},{7,6},{8,9},{9,8},{10,11... | collective-permute-start | bytes 12296 | tf_op jit(solution)/shard_map/ppermute | solution.py:180
  40.2 4.6 %collective-permute-start.1 = (f32[2,512]{1,0:T(2,128)S(1)}, f32[2,512]{1,0:T(2,128)S(1)}, u32[]{:S(2)}, u32[]{:S(2)}) collective-permute-start(f32[2,512]{1,0:T(2,128)S(1)} %fusion.33), channel_id=1, source_target_pairs={{0,2},{1,3},{2,0},{3,1},{4,6},{5,7},{6,4},{7,5},{8,10},{9,11},{10,... | collective-permute-start | bytes 12296 | tf_op jit(solution)/shard_map/ppermute | solution.py:184
  44.9 11.1 %collective-permute-start.2 = (f32[2,512]{1,0:T(2,128)S(1)}, f32[2,512]{1,0:T(2,128)S(1)}, u32[]{:S(2)}, u32[]{:S(2)}) collective-permute-start(f32[2,512]{1,0:T(2,128)S(1)} %add.105), channel_id=1, source_target_pairs={{0,4},{1,5},{2,6},{3,7},{4,0},{5,1},{6,2},{7,3},{8,12},{9,13},{10,... | collective-permute-start | bytes 12296 | tf_op jit(solution)/shard_map/ppermute | solution.py:187
  49.2 2.4 %copy-start.2 = (bf16[512,4608]{1,0:T(8,128)(2,1)S(1)}, bf16[512,4608]{1,0:T(8,128)(2,1)}, u32[]{:S(2)}) copy-start(bf16[512,4608]{1,0:T(8,128)(2,1)} %x_ref) | copy-start | bytes 14155780
  54.6 1.4 copy-start.9
  56.0 30.0 %collective-permute-start.11 = (bf16[16,144,512]{2,1,0:T(8,128)(2,1)}, bf16[16,144,512]{2,1,0:T(8,128)(2,1)}, u32[]{:S(2)}, u32[]{:S(2)}) collective-permute-start(bf16[16,144,512]{2,1,0:T(8,128)(2,1)} %get-tuple-element.22), channel_id=1, source_target_pairs={{0,8},{8,0},{16,24},{24,16},{32,40},{40,32},{48,56},{56,48},{64,72... | collective-permute-start | bytes 7077896 | tf_op jit(solution)/shard_map/ppermute | solution.py:199
  56.5 15.6 %collective-permute-start.3 = (bf16[512,512]{1,0:T(8,128)(2,1)S(1)}, bf16[512,512]{1,0:T(8,128)(2,1)S(1)}, u32[]{:S(2)}, u32[]{:S(2)}) collective-permute-start(bf16[512,512]{1,0:T(8,128)(2,1)S(1)} %multiply_convert_fusion.1.refs_2_), channel_id=1, source_target_pairs={{0,1},{1,2},{2,3},{3,4},{4,5},{5,6},{6,7},{7,0},{8,9},{9,10},{10,1... | collective-permute-start | bytes 1572872 | tf_op jit(solution)/shard_map/ppermute | solution.py:195
  57.0 15.0 %collective-permute-start.6 = (bf16[512,512]{1,0:T(8,128)(2,1)S(1)}, bf16[512,512]{1,0:T(8,128)(2,1)S(1)}, u32[]{:S(2)}, u32[]{:S(2)}) collective-permute-start(bf16[512,512]{1,0:T(8,128)(2,1)S(1)} %multiply_convert_fusion.1.refs_2_), channel_id=1, source_target_pairs={{0,7},{1,0},{2,1},{3,2},{4,3},{5,4},{6,5},{7,6},{8,15},{9,8},{10,9... | collective-permute-start | bytes 1572872 | tf_op jit(solution)/shard_map/ppermute | solution.py:195
  59.8 26.2 %collective-permute-start.12 = (bf16[512,512]{1,0:T(8,128)(2,1)S(1)}, bf16[512,512]{1,0:T(8,128)(2,1)}, u32[]{:S(2)}, u32[]{:S(2)}) collective-permute-start(bf16[512,512]{1,0:T(8,128)(2,1)S(1)} %multiply_convert_fusion.1.refs_2_), channel_id=1, source_target_pairs={{0,8},{8,0},{16,24},{24,16},{32,40},{40,32},{48,56},{56,48},{64,72... | collective-permute-start | bytes 1572872 | tf_op jit(solution)/shard_map/ppermute | solution.py:196
  72.1 21.0 %copy-start.4 = (bf16[512,512]{1,0:T(8,128)(2,1)}, bf16[512,512]{1,0:T(8,128)(2,1)S(1)}, u32[]{:S(2)}) copy-start(bf16[512,512]{1,0:T(8,128)(2,1)S(1)} %collective-permute-done.3.refs_3_) | copy-start | bytes 1572868
  72.1 21.0 %copy-start.6 = (bf16[512,512]{1,0:T(8,128)(2,1)}, bf16[512,512]{1,0:T(8,128)(2,1)S(1)}, u32[]{:S(2)}) copy-start(bf16[512,512]{1,0:T(8,128)(2,1)S(1)} %collective-permute-done.6.refs_4_) | copy-start | bytes 1572868
  72.1 13.7 %all-to-all-start.2 = ((f16[8,72,128]{2,1,0:T(8,128)(2,1)}), f16[8,72,128]{2,1,0:T(8,128)(2,1)S(1)}, u32[]{:S(2)}, u32[]{:S(2)}) async-start(f16[8,72,128]{2,1,0:T(8,128)(2,1)} %reshape.49), calls=%async_computation.2 | async-start | bytes 294912 | tf_op jit(solution)/shard_map/all_to_all | solution.py:210
  79.1 15.5 %collective-permute-start.4 = (bf16[512,512]{1,0:T(8,128)(2,1)S(1)}, bf16[512,512]{1,0:T(8,128)(2,1)S(1)}, u32[]{:S(2)}, u32[]{:S(2)}) collective-permute-start(bf16[512,512]{1,0:T(8,128)(2,1)S(1)} %collective-permute-done.3.refs_3_), channel_id=1, source_target_pairs={{0,1},{1,2},{2,3},{3,4},{4,5},{5,6},{6,7},{7,0},{8,9},{9,10},{10,1... | collective-permute-start | bytes 1572872 | tf_op jit(solution)/shard_map/ppermute | solution.py:206
  81.1 13.5 %collective-permute-start.7 = (bf16[512,512]{1,0:T(8,128)(2,1)S(1)}, bf16[512,512]{1,0:T(8,128)(2,1)S(1)}, u32[]{:S(2)}, u32[]{:S(2)}) collective-permute-start(bf16[512,512]{1,0:T(8,128)(2,1)S(1)} %collective-permute-done.6.refs_4_), channel_id=1, source_target_pairs={{0,7},{1,0},{2,1},{3,2},{4,3},{5,4},{6,5},{7,6},{8,15},{9,8},{10,9... | collective-permute-start | bytes 1572872 | tf_op jit(solution)/shard_map/ppermute | solution.py:206
  94.5 41.2 %all-to-all-start.3 = ((f16[16,144,512]{2,1,0:T(8,128)(2,1)}), f16[16,144,512]{2,1,0:T(8,128)(2,1)}, u32[]{:S(2)}, u32[]{:S(2)}) async-start(f16[16,144,512]{2,1,0:T(8,128)(2,1)} %multiply_convert_fusion), calls=%async_computation.3 | async-start | bytes 4718592 | tf_op jit(solution)/shard_map/all_to_all | solution.py:223
  101.8 13.9 %collective-permute-start.5 = (bf16[512,512]{1,0:T(8,128)(2,1)S(1)}, bf16[512,512]{1,0:T(8,128)(2,1)S(1)}, u32[]{:S(2)}, u32[]{:S(2)}) collective-permute-start(bf16[512,512]{1,0:T(8,128)(2,1)S(1)} %collective-permute-done.4.refs_5_), channel_id=1, source_target_pairs={{0,1},{1,2},{2,3},{3,4},{4,5},{5,6},{6,7},{7,0},{8,9},{9,10},{10,1... | collective-permute-start | bytes 1572872 | tf_op jit(solution)/shard_map/ppermute | solution.py:217
  103.2 2.5 %copy-start = (bf16[256,16,576]{2,1,0:T(8,128)(2,1)S(1)}, bf16[256,16,576]{2,1,0:T(8,128)(2,1)}, u32[]{:S(2)}) copy-start(bf16[256,16,576]{2,1,0:T(8,128)(2,1)} %all-gather.3.cloned.1.call-done) | copy-start | bytes 14155780
  105.7 1.0 copy-start.5
  106.7 1.0 copy-start.7
  110.5 11.9 %collective-permute-start.8 = (bf16[512,512]{1,0:T(8,128)(2,1)S(1)}, bf16[512,512]{1,0:T(8,128)(2,1)S(1)}, u32[]{:S(2)}, u32[]{:S(2)}) collective-permute-start(bf16[512,512]{1,0:T(8,128)(2,1)S(1)} %collective-permute-done.7.refs_6_), channel_id=1, source_target_pairs={{0,7},{1,0},{2,1},{3,2},{4,3},{5,4},{6,5},{7,6},{8,15},{9,8},{10,9... | collective-permute-start | bytes 1572872 | tf_op jit(solution)/shard_map/ppermute | solution.py:218
  115.7 11.1 %collective-permute-start.9 = (bf16[256,512]{1,0:T(8,128)(2,1)S(1)}, bf16[256,512]{1,0:T(8,128)(2,1)S(1)}, u32[]{:S(2)}, u32[]{:S(2)}) collective-permute-start(bf16[256,512]{1,0:T(8,128)(2,1)S(1)} %slice.16), channel_id=1, source_target_pairs={{0,1},{1,2},{2,3},{3,4},{4,5},{5,6},{6,7},{7,0},{8,9},{9,10},{10,1... | collective-permute-start | bytes 786440 | tf_op jit(solution)/shard_map/ppermute | solution.py:226
  122.4 7.7 %collective-permute-start.10 = (bf16[256,512]{1,0:T(8,128)(2,1)S(1)}, bf16[256,512]{1,0:T(8,128)(2,1)S(1)}, u32[]{:S(2)}, u32[]{:S(2)}) collective-permute-start(bf16[256,512]{1,0:T(8,128)(2,1)S(1)} %slice.17), channel_id=1, source_target_pairs={{0,7},{1,0},{2,1},{3,2},{4,3},{5,4},{6,5},{7,6},{8,15},{9,8},{10,9... | collective-permute-start | bytes 786440 | tf_op jit(solution)/shard_map/ppermute | solution.py:226
  130.1 2.5 %copy-start.1 = (bf16[256,16,576]{2,1,0:T(8,128)(2,1)S(1)}, bf16[256,16,576]{2,1,0:T(8,128)(2,1)}, u32[]{:S(2)}) copy-start(bf16[256,16,576]{2,1,0:T(8,128)(2,1)} %all-gather.3.cloned.1.call-done) | copy-start | bytes 14155780
Sparse Core Ops, SparseCore 0:
  28.0 53.6 all-gather.2

commit v4 on v3

--- a/solution.py
+++ b/solution.py
@@ -224,8 +224,9 @@
 
     half = tokens // 2
     up4, down4 = lax.ppermute(up3[:half], "vocab", z_shift(1)), lax.ppermute(down3[half:], "vocab", z_shift(-1))
+    emb_last = [lax.dynamic_index_in_dim(emb_cols, (z + d) % NZ, 1) for d in (5, 3, 4)]
     hidden_grad = hid_terms(
-        emb_cols, [z + 5, z + 3, z + 4], [up3, down3, jnp.concatenate([up4, down4], axis=0)], hid_sum
+        jnp.concatenate(emb_last, axis=1), [z * 0, z * 0 + 1, z * 0 + 2], [up3, down3, jnp.concatenate([up4, down4], axis=0)], hid_sum
     ).T
 
     embed_grad = (jnp.sum(after(tied, hidden_grad).astype(f32), axis=0) * (1.0 / emb_scale)).T

time: 146 us -> 144 us (0.986)
  waiting for transfers between devices: 32.7 us -> 30.8 us
    unnamed x22 -> x20, local copies, waits for them, and re-layouts: 11.5 us -> 9.02 us
    dynamic_slice x0 -> x1, local copies, waits for them, and re-layouts: none -> 1.66 us  [per_device(): lax.dynamic_index_in_dim(emb_cols, (z + d) % NZ, 1)]
  transfers between devices with their start and end apart: 18 -> 18, of which waited for: 9 -> 9; matrix products, arithmetic and copies ran while one was open for 14% -> 16% of each run, Pallas kernels for 10% -> 10%
where the time goes in v4:
time: 144 us; the launch traced here: 143 us
  starting transfers between devices  47.8 us (33%)
  waiting for transfers between devices  30.8 us (21%)
  matrix products  14.5 us (10%)
  between operations  14.3 us (10%)
  Pallas kernels  14.2 us (10%)
  local copies, waits for them, and re-layouts  13.5 us (9%)
  other arithmetic  7.68 us (5%)
    unnamed x20, local copies, waits for them, and re-layouts  9.02 us
    all_to_all x1, starting transfers between devices, per_device(): emb_few = lax.all_to_all(emb_few, 'vocab', 0, 0, tiled=True)  8.47 us
    all_to_all x1, starting transfers between devices, per_device(): packed = lax.all_to_all(packed, 'dp', 0, 0, tiled=True)  7.62 us
    dot_general x1, matrix products, per_device(): jnp.einsum('td,vd->tv', hidden, embedding, preferred_element_type=f32)  7.45 us
    all_to_all x1, starting transfers between devices, per_device(): lax.all_to_all(tied, 'dp', 0, 0, axis_index_groups=same_core, tiled=True)  7.18 us
    ppermute x1, waiting for transfers between devices, per_device(): lax.ppermute(scaled, 'vocab', z_shift(1))  7.14 us
    dot_general x1, matrix products, per_device(): jnp.einsum('kdt,tv->kdv', hid_pair, terms, preferred_element_type=f32)  7.09 us
    ppermute x1, waiting for transfers between devices, per_device(): down3 = lax.ppermute(after(down2, hid_sum), 'vocab', z_shift(-1))  6.58 us
  transfers between devices with their start and end apart: 18, of which 9 were waited for; matrix products, arithmetic and copies ran while one was open for 16% of the time, Pallas kernels for 10%

profile of v4, /device:TPU:2, one launch (start us, length us, event | category | flops | bytes accessed | tf_op | source)
XLA Modules:
  0.0 142.8 jit_solution(10604034039641721051)
XLA Ops:
  7.2 0.9 constant_dynamic-slice_fusion.3
  8.1 0.2 reshape.48
  8.3 0.7 copy.10
  8.9 8.5 %all-to-all-start.1 = ((bf16[8,16,576]{2,1,0:T(8,128)(2,1)}), bf16[8,16,576]{2,1,0:T(8,128)(2,1)S(1)}, u32[]{:S(2)}, u32[]{:S(2)}) async-start(bf16[8,16,576]{2,1,0:T(8,128)(2,1)} %copy.10), calls=%async_computation.1 | async-start | bytes 327680 | tf_op jit(solution)/shard_map/all_to_all | solution.py:172
  17.4 0.0 all-gather.3.cloned.1.call-start
  17.5 0.7 broadcast_subtract_fusion
  18.2 7.5 %exponential_reduce_fusion = (f32[512]{0:T(512)S(1)}, f32[512]{0:T(512)S(1)}, f32[512,512]{1,0:T(8,128)S(1)}) fusion(s32[512]{0:T(512)S(1)} %broadcast_subtract_fusion, bf16[512,4608]{1,0:T(8,128)(2,1)} %x_ref, bf16[512,4608]{1,0:T(8,128)(2,1)} %param.5), kind=kOutput, calls=%fused_computation.39 | convolution fusion | flops 2417490944 | bytes 10491904 | tf_op jit(solution)/shard_map/td,vd->tv/dot_general | solution.py:174
  25.6 1.6 %all-to-all-done.1 = bf16[8,16,576]{2,1,0:T(8,128)(2,1)S(1)} async-done(((bf16[8,16,576]{2,1,0:T(8,128)(2,1)}), bf16[8,16,576]{2,1,0:T(8,128)(2,1)S(1)}, u32[]{:S(2)}, u32[]{:S(2)}) %all-to-all-start.1) | async-done | bytes 147488 | tf_op jit(solution)/shard_map/all_to_all | solution.py:172
  27.2 0.7 copy-done.9
  27.8 0.0 all-gather.3.cloned.1.call-update
  27.9 1.0 shard_map.76
  28.9 7.6 %all-to-all-start = ((bf16[32,80,128]{2,1,0:T(8,128)(2,1)}), bf16[32,80,128]{2,1,0:T(8,128)(2,1)S(1)}, u32[]{:S(2)}, u32[]{:S(2)}) async-start(bf16[32,80,128]{2,1,0:T(8,128)(2,1)} %shard_map.76), calls=%async_computation | async-start | bytes 1310720 | tf_op jit(solution)/shard_map/all_to_all | solution.py:185
  36.5 0.7 collective-permute-start
  37.2 3.0 %collective-permute-done = f32[2,512]{1,0:T(2,128)S(1)} collective-permute-done((f32[2,512]{1,0:T(2,128)S(1)}, f32[2,512]{1,0:T(2,128)S(1)}, u32[]{:S(2)}, u32[]{:S(2)}) %collective-permute-start) | collective-permute-done | bytes 4128 | tf_op jit(solution)/shard_map/ppermute | solution.py:180
  40.2 1.4 collective-permute-start.1
  41.7 3.2 %collective-permute-done.1 = f32[2,512]{1,0:T(2,128)S(1)} collective-permute-done((f32[2,512]{1,0:T(2,128)S(1)}, f32[2,512]{1,0:T(2,128)S(1)}, u32[]{:S(2)}, u32[]{:S(2)}) %collective-permute-start.1) | collective-permute-done | bytes 4128 | tf_op jit(solution)/shard_map/ppermute | solution.py:184
  44.9 4.3 %collective-permute-start.2 = (f32[2,512]{1,0:T(2,128)S(1)}, f32[2,512]{1,0:T(2,128)S(1)}, u32[]{:S(2)}, u32[]{:S(2)}) collective-permute-start(f32[2,512]{1,0:T(2,128)S(1)} %add.118), channel_id=1, source_target_pairs={{0,4},{1,5},{2,6},{3,7},{4,0},{5,1},{6,2},{7,3},{8,12},{9,13},{10,... | collective-permute-start | bytes 12296 | tf_op jit(solution)/shard_map/ppermute | solution.py:187
  49.2 2.4 %copy-done.1 = bf16[512,4608]{1,0:T(8,128)(2,1)S(1)} copy-done((bf16[512,4608]{1,0:T(8,128)(2,1)S(1)}, bf16[512,4608]{1,0:T(8,128)(2,1)}, u32[]{:S(2)}) %copy-start.1) | copy-done | bytes 4718616
  51.6 3.0 %shard_map.79 = (bf16[16,144,512]{2,1,0:T(8,128)(2,1)S(1)}, bf16[16,144,512]{2,1,0:T(8,128)(2,1)}) custom-call(s32[1]{0:T(128)} %bitcast.14.core_ref, bf16[512,4608]{1,0:T(8,128)(2,1)S(1)} %copy-done.1), custom_call_target="tpu_custom_call" | custom-call | bytes 9437184 | tf_op jit(solution)/shard_map/pallas_call | solution.py:146
  54.6 1.4 copy-done.8
  56.0 0.0 collective-permute-start.11
  56.0 0.0 collective-permute-done.2
  56.0 0.0 all-to-all-done.x_ref
  56.0 0.4 multiply_convert_fusion.1.refs_2_
  56.5 0.6 collective-permute-start.3
  57.0 2.7 %collective-permute-start.6 = (bf16[512,512]{1,0:T(8,128)(2,1)S(1)}, bf16[512,512]{1,0:T(8,128)(2,1)S(1)}, u32[]{:S(2)}, u32[]{:S(2)}) collective-permute-start(bf16[512,512]{1,0:T(8,128)(2,1)S(1)} %multiply_convert_fusion.1.refs_2_), channel_id=1, source_target_pairs={{0,7},{1,0},{2,1},{3,2},{4,3},{5,4},{6,5},{7,6},{8,15},{9,8},{10,9... | collective-permute-start | bytes 1572872 | tf_op jit(solution)/shard_map/ppermute | solution.py:195
  59.8 0.0 collective-permute-start.12
  59.8 4.3 %shard_map.80 = f32[8,18,512]{2,1,0:T(8,128)S(1)} custom-call(bf16[32,80,128]{2,1,0:T(8,128)(2,1)S(1)} %all-to-all-done.x_ref), custom_call_target="tpu_custom_call" | custom-call | flops 5000000000 | bytes 2000000 | tf_op jit(solution)/shard_map/pallas_call | solution.py:57
  64.2 0.8 reshape.49
  64.9 7.1 %collective-permute-done.3.refs_3_ = bf16[512,512]{1,0:T(8,128)(2,1)S(1)} collective-permute-done((bf16[512,512]{1,0:T(8,128)(2,1)S(1)}, bf16[512,512]{1,0:T(8,128)(2,1)S(1)}, u32[]{:S(2)}, u32[]{:S(2)}) %collective-permute-start.3) | collective-permute-done | bytes 524320 | tf_op jit(solution)/shard_map/ppermute | solution.py:195
  72.1 0.0 collective-permute-done.6.refs_4_
  72.1 4.2 %all-to-all-start.2 = ((f16[8,72,128]{2,1,0:T(8,128)(2,1)}), f16[8,72,128]{2,1,0:T(8,128)(2,1)S(1)}, u32[]{:S(2)}, u32[]{:S(2)}) async-start(f16[8,72,128]{2,1,0:T(8,128)(2,1)} %reshape.49), calls=%async_computation.2 | async-start | bytes 294912 | tf_op jit(solution)/shard_map/all_to_all | solution.py:210
  76.3 2.7 %select_convert_fusion = bf16[16,144,288]{2,1,0:T(8,128)(2,1)} fusion(s32[]{:T(128)S(6)} %mul.63, s32[]{:T(128)S(6)} %select_n.110, s32[288]{0:T(512)S(1)} %get-tuple-element.37, s32[288]{0:T(512)S(1)} %get-tuple-element.38, s32[16,144]{1,0:T(8,128)S(1)} %multiply_add_fusion, pred[288]{0:T(512)(128)(4,1)S(1)} %fusion.31), kind=kLoop, calls=%fused_computation.22 | loop fusion | flops 13934592 | bytes 1338920 | tf_op jit(solution)/shard_map/convert_element_type | solution.py:203
  79.1 2.0 %collective-permute-start.4 = (bf16[512,512]{1,0:T(8,128)(2,1)S(1)}, bf16[512,512]{1,0:T(8,128)(2,1)S(1)}, u32[]{:S(2)}, u32[]{:S(2)}) collective-permute-start(bf16[512,512]{1,0:T(8,128)(2,1)S(1)} %collective-permute-done.3.refs_3_), channel_id=1, source_target_pairs={{0,1},{1,2},{2,3},{3,4},{4,5},{5,6},{6,7},{7,0},{8,9},{9,10},{10,1... | collective-permute-start | bytes 1572872 | tf_op jit(solution)/shard_map/ppermute | solution.py:206
  81.1 1.2 collective-permute-start.7
  82.3 3.5 %all-to-all-done.2 = f16[8,72,128]{2,1,0:T(8,128)(2,1)S(1)} async-done(((f16[8,72,128]{2,1,0:T(8,128)(2,1)}), f16[8,72,128]{2,1,0:T(8,128)(2,1)S(1)}, u32[]{:S(2)}, u32[]{:S(2)}) %all-to-all-start.2) | async-done | bytes 147488 | tf_op jit(solution)/shard_map/all_to_all | solution.py:210
  85.9 0.1 convert_element_type.42
  86.0 0.0 collective-permute-done.12
  86.0 0.0 collective-permute-done.11
  86.0 7.1 %multiply_convert_fusion = f16[16,144,512]{2,1,0:T(8,128)(2,1)} fusion(bf16[16,144,288]{2,1,0:T(8,128)(2,1)} %select_convert_fusion, bf16[16,144,512]{2,1,0:T(8,128)(2,1)} %collective-permute-done.11, bf16[16,144,512]{2,1,0:T(8,128)(2,1)} %copy-done.8, bf16[144,512]{1,0:T(8,128)(2,1)S(1)} %subtract_convert_fusion, ...), kind=kOutput, calls=%fused_computation.15 | convolution fusion | flops 3121266688 | bytes 9748480 | tf_op jit(solution)/shard_map/kdt,tv->kdv/dot_general | solution.py:221
  93.1 0.0 copy-done.3
  93.1 1.4 collective-permute-done.4.refs_5_
  94.5 0.0 collective-permute-done.7.refs_6_
  94.5 7.2 %all-to-all-start.3 = ((f16[16,144,512]{2,1,0:T(8,128)(2,1)}), f16[16,144,512]{2,1,0:T(8,128)(2,1)}, u32[]{:S(2)}, u32[]{:S(2)}) async-start(f16[16,144,512]{2,1,0:T(8,128)(2,1)} %multiply_convert_fusion), calls=%async_computation.3 | async-start | bytes 4718592 | tf_op jit(solution)/shard_map/all_to_all | solution.py:223
  101.7 0.1 stack.42.refs_0_
  101.8 1.4 collective-permute-start.5
  103.2 2.5 %copy-done = bf16[256,16,576]{2,1,0:T(8,128)(2,1)S(1)} copy-done((bf16[256,16,576]{2,1,0:T(8,128)(2,1)S(1)}, bf16[256,16,576]{2,1,0:T(8,128)(2,1)}, u32[]{:S(2)}) %copy-start) | copy-done | bytes 4718616
  105.7 1.0 copy-done.4
  106.7 1.0 copy-done.6
  107.7 2.8 %shard_map.77.refs_5_ = f32[512,576]{1,0:T(8,128)S(1)} custom-call(s32[5]{0:T(128)S(1)} %stack.42.refs_0_, bf16[32,8,16,576]{3,2,1,0:T(8,128)(2,1)S(1)} %bitcast.23, bf16[512,512]{1,0:T(8,128)(2,1)S(1)} %multiply_convert_fusion.1.refs_2_, bf16[512,512]{1,0:T(8,128)(2,1)S(1)} %copy-done.4, bf16[512,512]{1,0:T(8,128)(2,1)S(1)} %copy-done.6, ...), custom_call_target="tpu_custom_call" | custom-call | flops 1509949440 | bytes 8388608 | tf_op jit(solution)/shard_map/pallas_call | solution.py:93
  110.5 2.1 %collective-permute-start.8 = (bf16[512,512]{1,0:T(8,128)(2,1)S(1)}, bf16[512,512]{1,0:T(8,128)(2,1)S(1)}, u32[]{:S(2)}, u32[]{:S(2)}) collective-permute-start(bf16[512,512]{1,0:T(8,128)(2,1)S(1)} %collective-permute-done.7.refs_6_), channel_id=1, source_target_pairs={{0,7},{1,0},{2,1},{3,2},{4,3},{5,4},{6,5},{7,6},{8,15},{9,8},{10,9... | collective-permute-start | bytes 1572872 | tf_op jit(solution)/shard_map/ppermute | solution.py:218
  112.6 0.6 log_subtract_fusion
  113.2 2.5 %collective-permute-done.5.refs_2_ = bf16[512,512]{1,0:T(8,128)(2,1)S(1)} collective-permute-done((bf16[512,512]{1,0:T(8,128)(2,1)S(1)}, bf16[512,512]{1,0:T(8,128)(2,1)S(1)}, u32[]{:S(2)}, u32[]{:S(2)}) %collective-permute-start.5) | collective-permute-done | bytes 524320 | tf_op jit(solution)/shard_map/ppermute | solution.py:217
  115.7 0.1 collective-permute-start.9
  115.8 6.6 %collective-permute-done.8.refs_3_ = bf16[512,512]{1,0:T(8,128)(2,1)S(1)} collective-permute-done((bf16[512,512]{1,0:T(8,128)(2,1)S(1)}, bf16[512,512]{1,0:T(8,128)(2,1)S(1)}, u32[]{:S(2)}, u32[]{:S(2)}) %collective-permute-start.8) | collective-permute-done | bytes 524320 | tf_op jit(solution)/shard_map/ppermute | solution.py:218
  122.4 3.8 %collective-permute-start.10 = (bf16[256,512]{1,0:T(8,128)(2,1)S(1)}, bf16[256,512]{1,0:T(8,128)(2,1)S(1)}, u32[]{:S(2)}, u32[]{:S(2)}) collective-permute-start(bf16[256,512]{1,0:T(8,128)(2,1)S(1)} %slice.17), channel_id=1, source_target_pairs={{0,7},{1,0},{2,1},{3,2},{4,3},{5,4},{6,5},{7,6},{8,15},{9,8},{10,9... | collective-permute-start | bytes 786440 | tf_op jit(solution)/shard_map/ppermute | solution.py:226
  126.2 1.7 %constant_dynamic-slice_fusion.2 = (bf16[32,1,16,576]{3,2,1,0:T(8,128)(2,1)S(1)}, bf16[32,1,16,576]{3,2,1,0:T(8,128)(2,1)S(1)}, bf16[32,1,16,576]{3,2,1,0:T(8,128)(2,1)S(1)}) fusion(bf16[32,8,16,576]{3,2,1,0:T(8,128)(2,1)} %bitcast.22, s32[]{:T(128)S(6)} %select_n.96, s32[]{:T(128)S(6)} %select_n.100, s32[]{:T(128)S(6)} %select_n.98), kind=kLoop, calls=%fused_computation.54 | loop fusion | bytes 3538956 | tf_op jit(solution)/shard_map/jit(dynamic_index_in_dim)/dynamic_slice | solution.py:227
  127.8 0.3 pad_maximum_fusion.refs_1_
  128.1 0.0 collective-permute-done.9
  128.2 1.9 %collective-permute-done.10 = bf16[256,512]{1,0:T(8,128)(2,1)S(1)} collective-permute-done((bf16[256,512]{1,0:T(8,128)(2,1)S(1)}, bf16[256,512]{1,0:T(8,128)(2,1)S(1)}, u32[]{:S(2)}, u32[]{:S(2)}) %collective-permute-start.10) | collective-permute-done | bytes 262176 | tf_op jit(solution)/shard_map/ppermute | solution.py:226
  130.1 3.1 %shard_map.78 = f32[576,512]{1,0:T(8,128)} custom-call(s32[3]{0:T(128)S(1)} %stack.36.refs_0_, bf16[32,3,16,576]{3,2,1,0:T(8,128)(2,1)S(1)} %pad_maximum_fusion.refs_1_, bf16[512,512]{1,0:T(8,128)(2,1)S(1)} %collective-permute-done.5.refs_2_, bf16[512,512]{1,0:T(8,128)(2,1)S(1)} %collective-permute-done.8.refs_3_, ...), custom_call_target="tpu_custom_call" | custom-call | flops 905969664 | bytes 8388608 | tf_op jit(solution)/shard_map/pallas_call | solution.py:93
  133.2 0.0 all-to-all-done.3
  133.2 2.0 %convert_reduce_fusion = f32[144,512]{1,0:T(8,128)S(1)} fusion(f16[16,144,512]{2,1,0:T(8,128)(2,1)} %all-to-all-done.3), kind=kLoop, calls=%fused_computation.14 | loop fusion | flops 2285568 | bytes 2654208 | tf_op jit(solution)/shard_map/reduce_sum | solution.py:232
  135.2 0.7 multiply_bitcast_fusion
  (30 shorter events, 0.3 us)
Async XLA Ops:
  8.9 18.2 %all-to-all-start.1 = ((bf16[8,16,576]{2,1,0:T(8,128)(2,1)}), bf16[8,16,576]{2,1,0:T(8,128)(2,1)S(1)}, u32[]{:S(2)}, u32[]{:S(2)}) async-start(bf16[8,16,576]{2,1,0:T(8,128)(2,1)} %copy.10), calls=%async_computation.1 | async-start | bytes 327680 | tf_op jit(solution)/shard_map/all_to_all | solution.py:172
  17.4 85.8 %all-gather.3.cloned.1.call-start = ((), (), s32[]{:S(2)}) async-start(), calls=%async_computation.4 | async-start | bytes 5406720 | tf_op jit(solution)/shard_map/all_gather | solution.py:181
  18.1 9.7 %copy-start.2 = (bf16[512,576]{0,1:T(8,128)(2,1)S(1)}, bf16[512,576]{0,1:T(8,128)(2,1)}, u32[]{:S(2)}) copy-start(bf16[512,576]{0,1:T(8,128)(2,1)} %param.9) | copy-start | bytes 1769476
  18.1 9.7 %copy-start.7 = (s32[512]{0:T(512)S(1)}, s32[512]{0:T(512)}, u32[]{:S(2)}) copy-start(s32[512]{0:T(512)} %param.8) | copy-start | bytes 6148
  27.2 0.7 copy-start.9
  28.9 27.1 %all-to-all-start = ((bf16[32,80,128]{2,1,0:T(8,128)(2,1)}), bf16[32,80,128]{2,1,0:T(8,128)(2,1)S(1)}, u32[]{:S(2)}, u32[]{:S(2)}) async-start(bf16[32,80,128]{2,1,0:T(8,128)(2,1)} %shard_map.76), calls=%async_computation | async-start | bytes 1310720 | tf_op jit(solution)/shard_map/all_to_all | solution.py:185
  36.5 3.7 %collective-permute-start = (f32[2,512]{1,0:T(2,128)S(1)}, f32[2,512]{1,0:T(2,128)S(1)}, u32[]{:S(2)}, u32[]{:S(2)}) collective-permute-start(f32[2,512]{1,0:T(2,128)S(1)} %pad_maximum_fusion.2), channel_id=1, source_target_pairs={{0,1},{1,0},{2,3},{3,2},{4,5},{5,4},{6,7},{7,6},{8,9},{9,8},{10,11... | collective-permute-start | bytes 12296 | tf_op jit(solution)/shard_map/ppermute | solution.py:180
  40.2 4.6 %collective-permute-start.1 = (f32[2,512]{1,0:T(2,128)S(1)}, f32[2,512]{1,0:T(2,128)S(1)}, u32[]{:S(2)}, u32[]{:S(2)}) collective-permute-start(f32[2,512]{1,0:T(2,128)S(1)} %fusion.33), channel_id=1, source_target_pairs={{0,2},{1,3},{2,0},{3,1},{4,6},{5,7},{6,4},{7,5},{8,10},{9,11},{10,... | collective-permute-start | bytes 12296 | tf_op jit(solution)/shard_map/ppermute | solution.py:184
  44.9 11.1 %collective-permute-start.2 = (f32[2,512]{1,0:T(2,128)S(1)}, f32[2,512]{1,0:T(2,128)S(1)}, u32[]{:S(2)}, u32[]{:S(2)}) collective-permute-start(f32[2,512]{1,0:T(2,128)S(1)} %add.118), channel_id=1, source_target_pairs={{0,4},{1,5},{2,6},{3,7},{4,0},{5,1},{6,2},{7,3},{8,12},{9,13},{10,... | collective-permute-start | bytes 12296 | tf_op jit(solution)/shard_map/ppermute | solution.py:187
  49.2 2.4 %copy-start.1 = (bf16[512,4608]{1,0:T(8,128)(2,1)S(1)}, bf16[512,4608]{1,0:T(8,128)(2,1)}, u32[]{:S(2)}) copy-start(bf16[512,4608]{1,0:T(8,128)(2,1)} %x_ref) | copy-start | bytes 14155780
  54.6 1.4 copy-start.8
  56.0 30.0 %collective-permute-start.11 = (bf16[16,144,512]{2,1,0:T(8,128)(2,1)}, bf16[16,144,512]{2,1,0:T(8,128)(2,1)}, u32[]{:S(2)}, u32[]{:S(2)}) collective-permute-start(bf16[16,144,512]{2,1,0:T(8,128)(2,1)} %get-tuple-element.22), channel_id=1, source_target_pairs={{0,8},{8,0},{16,24},{24,16},{32,40},{40,32},{48,56},{56,48},{64,72... | collective-permute-start | bytes 7077896 | tf_op jit(solution)/shard_map/ppermute | solution.py:199
  56.5 15.6 %collective-permute-start.3 = (bf16[512,512]{1,0:T(8,128)(2,1)S(1)}, bf16[512,512]{1,0:T(8,128)(2,1)S(1)}, u32[]{:S(2)}, u32[]{:S(2)}) collective-permute-start(bf16[512,512]{1,0:T(8,128)(2,1)S(1)} %multiply_convert_fusion.1.refs_2_), channel_id=1, source_target_pairs={{0,1},{1,2},{2,3},{3,4},{4,5},{5,6},{6,7},{7,0},{8,9},{9,10},{10,1... | collective-permute-start | bytes 1572872 | tf_op jit(solution)/shard_map/ppermute | solution.py:195
  57.0 15.0 %collective-permute-start.6 = (bf16[512,512]{1,0:T(8,128)(2,1)S(1)}, bf16[512,512]{1,0:T(8,128)(2,1)S(1)}, u32[]{:S(2)}, u32[]{:S(2)}) collective-permute-start(bf16[512,512]{1,0:T(8,128)(2,1)S(1)} %multiply_convert_fusion.1.refs_2_), channel_id=1, source_target_pairs={{0,7},{1,0},{2,1},{3,2},{4,3},{5,4},{6,5},{7,6},{8,15},{9,8},{10,9... | collective-permute-start | bytes 1572872 | tf_op jit(solution)/shard_map/ppermute | solution.py:195
  59.8 26.2 %collective-permute-start.12 = (bf16[512,512]{1,0:T(8,128)(2,1)S(1)}, bf16[512,512]{1,0:T(8,128)(2,1)}, u32[]{:S(2)}, u32[]{:S(2)}) collective-permute-start(bf16[512,512]{1,0:T(8,128)(2,1)S(1)} %multiply_convert_fusion.1.refs_2_), channel_id=1, source_target_pairs={{0,8},{8,0},{16,24},{24,16},{32,40},{40,32},{48,56},{56,48},{64,72... | collective-permute-start | bytes 1572872 | tf_op jit(solution)/shard_map/ppermute | solution.py:196
  72.1 21.0 %copy-start.3 = (bf16[512,512]{1,0:T(8,128)(2,1)}, bf16[512,512]{1,0:T(8,128)(2,1)S(1)}, u32[]{:S(2)}) copy-start(bf16[512,512]{1,0:T(8,128)(2,1)S(1)} %collective-permute-done.3.refs_3_) | copy-start | bytes 1572868
  72.1 21.0 %copy-start.5 = (bf16[512,512]{1,0:T(8,128)(2,1)}, bf16[512,512]{1,0:T(8,128)(2,1)S(1)}, u32[]{:S(2)}) copy-start(bf16[512,512]{1,0:T(8,128)(2,1)S(1)} %collective-permute-done.6.refs_4_) | copy-start | bytes 1572868
  72.1 13.7 %all-to-all-start.2 = ((f16[8,72,128]{2,1,0:T(8,128)(2,1)}), f16[8,72,128]{2,1,0:T(8,128)(2,1)S(1)}, u32[]{:S(2)}, u32[]{:S(2)}) async-start(f16[8,72,128]{2,1,0:T(8,128)(2,1)} %reshape.49), calls=%async_computation.2 | async-start | bytes 294912 | tf_op jit(solution)/shard_map/all_to_all | solution.py:210
  79.1 15.5 %collective-permute-start.4 = (bf16[512,512]{1,0:T(8,128)(2,1)S(1)}, bf16[512,512]{1,0:T(8,128)(2,1)S(1)}, u32[]{:S(2)}, u32[]{:S(2)}) collective-permute-start(bf16[512,512]{1,0:T(8,128)(2,1)S(1)} %collective-permute-done.3.refs_3_), channel_id=1, source_target_pairs={{0,1},{1,2},{2,3},{3,4},{4,5},{5,6},{6,7},{7,0},{8,9},{9,10},{10,1... | collective-permute-start | bytes 1572872 | tf_op jit(solution)/shard_map/ppermute | solution.py:206
  81.1 13.5 %collective-permute-start.7 = (bf16[512,512]{1,0:T(8,128)(2,1)S(1)}, bf16[512,512]{1,0:T(8,128)(2,1)S(1)}, u32[]{:S(2)}, u32[]{:S(2)}) collective-permute-start(bf16[512,512]{1,0:T(8,128)(2,1)S(1)} %collective-permute-done.6.refs_4_), channel_id=1, source_target_pairs={{0,7},{1,0},{2,1},{3,2},{4,3},{5,4},{6,5},{7,6},{8,15},{9,8},{10,9... | collective-permute-start | bytes 1572872 | tf_op jit(solution)/shard_map/ppermute | solution.py:206
  94.5 38.7 %all-to-all-start.3 = ((f16[16,144,512]{2,1,0:T(8,128)(2,1)}), f16[16,144,512]{2,1,0:T(8,128)(2,1)}, u32[]{:S(2)}, u32[]{:S(2)}) async-start(f16[16,144,512]{2,1,0:T(8,128)(2,1)} %multiply_convert_fusion), calls=%async_computation.3 | async-start | bytes 4718592 | tf_op jit(solution)/shard_map/all_to_all | solution.py:223
  101.8 13.9 %collective-permute-start.5 = (bf16[512,512]{1,0:T(8,128)(2,1)S(1)}, bf16[512,512]{1,0:T(8,128)(2,1)S(1)}, u32[]{:S(2)}, u32[]{:S(2)}) collective-permute-start(bf16[512,512]{1,0:T(8,128)(2,1)S(1)} %collective-permute-done.4.refs_5_), channel_id=1, source_target_pairs={{0,1},{1,2},{2,3},{3,4},{4,5},{5,6},{6,7},{7,0},{8,9},{9,10},{10,1... | collective-permute-start | bytes 1572872 | tf_op jit(solution)/shard_map/ppermute | solution.py:217
  103.2 2.5 %copy-start = (bf16[256,16,576]{2,1,0:T(8,128)(2,1)S(1)}, bf16[256,16,576]{2,1,0:T(8,128)(2,1)}, u32[]{:S(2)}) copy-start(bf16[256,16,576]{2,1,0:T(8,128)(2,1)} %all-gather.3.cloned.1.call-done) | copy-start | bytes 14155780
  105.7 1.0 copy-start.4
  106.7 1.0 copy-start.6
  110.5 11.9 %collective-permute-start.8 = (bf16[512,512]{1,0:T(8,128)(2,1)S(1)}, bf16[512,512]{1,0:T(8,128)(2,1)S(1)}, u32[]{:S(2)}, u32[]{:S(2)}) collective-permute-start(bf16[512,512]{1,0:T(8,128)(2,1)S(1)} %collective-permute-done.7.refs_6_), channel_id=1, source_target_pairs={{0,7},{1,0},{2,1},{3,2},{4,3},{5,4},{6,5},{7,6},{8,15},{9,8},{10,9... | collective-permute-start | bytes 1572872 | tf_op jit(solution)/shard_map/ppermute | solution.py:218
  115.7 12.5 %collective-permute-start.9 = (bf16[256,512]{1,0:T(8,128)(2,1)S(1)}, bf16[256,512]{1,0:T(8,128)(2,1)S(1)}, u32[]{:S(2)}, u32[]{:S(2)}) collective-permute-start(bf16[256,512]{1,0:T(8,128)(2,1)S(1)} %slice.16), channel_id=1, source_target_pairs={{0,1},{1,2},{2,3},{3,4},{4,5},{5,6},{6,7},{7,0},{8,9},{9,10},{10,1... | collective-permute-start | bytes 786440 | tf_op jit(solution)/shard_map/ppermute | solution.py:226
  122.4 7.7 %collective-permute-start.10 = (bf16[256,512]{1,0:T(8,128)(2,1)S(1)}, bf16[256,512]{1,0:T(8,128)(2,1)S(1)}, u32[]{:S(2)}, u32[]{:S(2)}) collective-permute-start(bf16[256,512]{1,0:T(8,128)(2,1)S(1)} %slice.17), channel_id=1, source_target_pairs={{0,7},{1,0},{2,1},{3,2},{4,3},{5,4},{6,5},{7,6},{8,15},{9,8},{10,9... | collective-permute-start | bytes 786440 | tf_op jit(solution)/shard_map/ppermute | solution.py:226
Sparse Core Ops, SparseCore 0:
  28.0 53.6 all-gather.2

commit v5 on v4

--- a/solution.py
+++ b/solution.py
@@ -229,7 +229,7 @@
         jnp.concatenate(emb_last, axis=1), [z * 0, z * 0 + 1, z * 0 + 2], [up3, down3, jnp.concatenate([up4, down4], axis=0)], hid_sum
     ).T
 
-    embed_grad = (jnp.sum(after(tied, hidden_grad).astype(f32), axis=0) * (1.0 / emb_scale)).T
+    embed_grad = (jnp.sum(tied.astype(f32), axis=0) * (1.0 / emb_scale)).T
     return (token_loss, hidden_grad, embed_grad)
 
 

time: 144 us -> 154 us (1.069)
  waiting for transfers between devices: 30.8 us -> 43.1 us
  starting transfers between devices: 47.8 us -> 44.2 us
    all_to_all x1, waiting for transfers between devices: 0.01 us -> 15.7 us  [per_device(): lax.all_to_all(tied, 'dp', 0, 0, axis_index_groups=same_core, tiled=True)]
    ppermute x1, waiting for transfers between devices: 6.58 us -> 0.01 us  [per_device(): down3 = lax.ppermute(after(down2, hid_sum), 'vocab', z_shift(-1))]
    ppermute x1, starting transfers between devices: 3.77 us -> 0.08 us  [per_device(): lax.ppermute(down3[half:], 'vocab', z_shift(-1))]
    ppermute x1, waiting for transfers between devices: 1.9 us -> 4.35 us  [per_device(): lax.ppermute(down3[half:], 'vocab', z_shift(-1))]
    all_to_all x1, waiting for transfers between devices: 3.48 us -> 5.9 us  [per_device(): lax.all_to_all(after(sums, up1, down1), 'vocab', 0, 0, tiled=True)]
    unnamed x20 -> x12, local copies, waits for them, and re-layouts: 9.02 us -> 6.92 us
    convert_element_type x1, other arithmetic: 2.73 us -> 0.8 us  [per_device(): jnp.where(row == place, 1.0 / emb_scale, 0.0).astype(bf16)]
    convert_element_type x1, local copies, waits for them, and re-layouts: 0.05 us -> 1.72 us  [per_device(): sums_low = (sums.astype(f32) - sums_high.astype(f32)).astype(bf16)]
  transfers between devices with their start and end apart: 18 -> 18, of which waited for: 9 -> 8; matrix products, arithmetic and copies ran while one was open for 16% -> 18% of each run, Pallas kernels for 10% -> 8%
where the time goes in v5:
time: 154 us; the launch traced here: 152 us
  starting transfers between devices  44.2 us (29%)
  waiting for transfers between devices  43.1 us (28%)
  Pallas kernels  14.9 us (10%)
  matrix products  14.3 us (9%)
  between operations  14.2 us (9%)
  local copies, waits for them, and re-layouts  14 us (9%)
  other arithmetic  7.46 us (5%)
    all_to_all x1, waiting for transfers between devices, per_device(): lax.all_to_all(tied, 'dp', 0, 0, axis_index_groups=same_core, tiled=True)  15.7 us
    all_to_all x1, starting transfers between devices, per_device(): emb_few = lax.all_to_all(emb_few, 'vocab', 0, 0, tiled=True)  8.47 us
    all_to_all x1, starting transfers between devices, per_device(): packed = lax.all_to_all(packed, 'dp', 0, 0, tiled=True)  7.62 us
    dot_general x1, matrix products, per_device(): jnp.einsum('td,vd->tv', hidden, embedding, preferred_element_type=f32)  7.45 us
    all_to_all x1, starting transfers between devices, per_device(): lax.all_to_all(tied, 'dp', 0, 0, axis_index_groups=same_core, tiled=True)  7.25 us
    ppermute x1, waiting for transfers between devices, per_device(): lax.ppermute(scaled, 'vocab', z_shift(1))  7.13 us
    unnamed x12, local copies, waits for them, and re-layouts  6.92 us
    dot_general x1, matrix products, per_device(): jnp.einsum('kdt,tv->kdv', hid_pair, terms, preferred_element_type=f32)  6.82 us
  transfers between devices with their start and end apart: 18, of which 8 were waited for; matrix products, arithmetic and copies ran while one was open for 18% of the time, Pallas kernels for 8%

profile of v5, /device:TPU:2, one launch (start us, length us, event | category | flops | bytes accessed | tf_op | source)
XLA Modules:
  0.0 152.2 jit_solution(8330415731416200528)
XLA Ops:
  7.2 0.9 constant_dynamic-slice_fusion.3
  8.1 0.2 reshape.48
  8.3 0.7 copy.10
  8.9 8.5 %all-to-all-start.1 = ((bf16[8,16,576]{2,1,0:T(8,128)(2,1)}), bf16[8,16,576]{2,1,0:T(8,128)(2,1)S(1)}, u32[]{:S(2)}, u32[]{:S(2)}) async-start(bf16[8,16,576]{2,1,0:T(8,128)(2,1)} %copy.10), calls=%async_computation.1 | async-start | bytes 327680 | tf_op jit(solution)/shard_map/all_to_all | solution.py:172
  17.4 0.0 all-gather.3.cloned.1.call-start
  17.5 0.7 broadcast_subtract_fusion
  18.2 7.4 %exponential_reduce_fusion = (f32[512]{0:T(512)S(1)}, f32[512]{0:T(512)S(1)}, f32[512,512]{1,0:T(8,128)S(1)}) fusion(s32[512]{0:T(512)S(1)} %broadcast_subtract_fusion, bf16[512,4608]{1,0:T(8,128)(2,1)} %x_ref, bf16[512,4608]{1,0:T(8,128)(2,1)} %param.5), kind=kOutput, calls=%fused_computation.39 | convolution fusion | flops 2417490944 | bytes 10491904 | tf_op jit(solution)/shard_map/td,vd->tv/dot_general | solution.py:174
  25.6 1.6 %all-to-all-done.1 = bf16[8,16,576]{2,1,0:T(8,128)(2,1)S(1)} async-done(((bf16[8,16,576]{2,1,0:T(8,128)(2,1)}), bf16[8,16,576]{2,1,0:T(8,128)(2,1)S(1)}, u32[]{:S(2)}, u32[]{:S(2)}) %all-to-all-start.1) | async-done | bytes 147488 | tf_op jit(solution)/shard_map/all_to_all | solution.py:172
  27.2 0.7 copy-done.5
  27.8 0.0 all-gather.3.cloned.1.call-update
  27.9 1.0 shard_map.76
  28.9 7.6 %all-to-all-start = ((bf16[32,80,128]{2,1,0:T(8,128)(2,1)}), bf16[32,80,128]{2,1,0:T(8,128)(2,1)S(1)}, u32[]{:S(2)}, u32[]{:S(2)}) async-start(bf16[32,80,128]{2,1,0:T(8,128)(2,1)} %shard_map.76), calls=%async_computation | async-start | bytes 1310720 | tf_op jit(solution)/shard_map/all_to_all | solution.py:185
  36.5 0.7 collective-permute-start
  37.2 3.0 %collective-permute-done = f32[2,512]{1,0:T(2,128)S(1)} collective-permute-done((f32[2,512]{1,0:T(2,128)S(1)}, f32[2,512]{1,0:T(2,128)S(1)}, u32[]{:S(2)}, u32[]{:S(2)}) %collective-permute-start) | collective-permute-done | bytes 4128 | tf_op jit(solution)/shard_map/ppermute | solution.py:180
  40.2 1.4 collective-permute-start.1
  41.6 3.2 %collective-permute-done.1 = f32[2,512]{1,0:T(2,128)S(1)} collective-permute-done((f32[2,512]{1,0:T(2,128)S(1)}, f32[2,512]{1,0:T(2,128)S(1)}, u32[]{:S(2)}, u32[]{:S(2)}) %collective-permute-start.1) | collective-permute-done | bytes 4128 | tf_op jit(solution)/shard_map/ppermute | solution.py:184
  44.9 4.3 %collective-permute-start.2 = (f32[2,512]{1,0:T(2,128)S(1)}, f32[2,512]{1,0:T(2,128)S(1)}, u32[]{:S(2)}, u32[]{:S(2)}) collective-permute-start(f32[2,512]{1,0:T(2,128)S(1)} %add.118), channel_id=1, source_target_pairs={{0,4},{1,5},{2,6},{3,7},{4,0},{5,1},{6,2},{7,3},{8,12},{9,13},{10,... | collective-permute-start | bytes 12296 | tf_op jit(solution)/shard_map/ppermute | solution.py:187
  49.2 2.4 %copy-done.1 = bf16[512,4608]{1,0:T(8,128)(2,1)S(1)} copy-done((bf16[512,4608]{1,0:T(8,128)(2,1)S(1)}, bf16[512,4608]{1,0:T(8,128)(2,1)}, u32[]{:S(2)}) %copy-start.1) | copy-done | bytes 4718616
  51.6 3.0 %shard_map.79 = (bf16[16,144,512]{2,1,0:T(8,128)(2,1)S(1)}, bf16[16,144,512]{2,1,0:T(8,128)(2,1)}) custom-call(s32[1]{0:T(128)} %bitcast.14.core_ref, bf16[512,4608]{1,0:T(8,128)(2,1)S(1)} %copy-done.1), custom_call_target="tpu_custom_call" | custom-call | bytes 9437184 | tf_op jit(solution)/shard_map/pallas_call | solution.py:146
  54.6 1.4 copy-done.4
  56.0 0.0 collective-permute-start.11
  56.0 0.0 collective-permute-done.2
  56.0 0.0 all-to-all-done.x_ref
  56.0 0.4 multiply_convert_fusion.1.refs_2_
  56.5 0.6 collective-permute-start.3
  57.0 2.7 %collective-permute-start.6 = (bf16[512,512]{1,0:T(8,128)(2,1)S(1)}, bf16[512,512]{1,0:T(8,128)(2,1)S(1)}, u32[]{:S(2)}, u32[]{:S(2)}) collective-permute-start(bf16[512,512]{1,0:T(8,128)(2,1)S(1)} %multiply_convert_fusion.1.refs_2_), channel_id=1, source_target_pairs={{0,7},{1,0},{2,1},{3,2},{4,3},{5,4},{6,5},{7,6},{8,15},{9,8},{10,9... | collective-permute-start | bytes 1572872 | tf_op jit(solution)/shard_map/ppermute | solution.py:195
  59.8 0.0 collective-permute-start.12
  59.8 4.3 %shard_map.80 = f32[8,18,512]{2,1,0:T(8,128)S(1)} custom-call(bf16[32,80,128]{2,1,0:T(8,128)(2,1)S(1)} %all-to-all-done.x_ref), custom_call_target="tpu_custom_call" | custom-call | flops 5000000000 | bytes 2000000 | tf_op jit(solution)/shard_map/pallas_call | solution.py:57
  64.2 0.8 reshape.49
  64.9 7.1 %collective-permute-done.3.refs_3_ = bf16[512,512]{1,0:T(8,128)(2,1)S(1)} collective-permute-done((bf16[512,512]{1,0:T(8,128)(2,1)S(1)}, bf16[512,512]{1,0:T(8,128)(2,1)S(1)}, u32[]{:S(2)}, u32[]{:S(2)}) %collective-permute-start.3) | collective-permute-done | bytes 524320 | tf_op jit(solution)/shard_map/ppermute | solution.py:195
  72.1 0.0 collective-permute-done.6.refs_4_
  72.1 4.2 %all-to-all-start.2 = ((f16[8,72,128]{2,1,0:T(8,128)(2,1)}), f16[8,72,128]{2,1,0:T(8,128)(2,1)S(1)}, u32[]{:S(2)}, u32[]{:S(2)}) async-start(f16[8,72,128]{2,1,0:T(8,128)(2,1)} %reshape.49), calls=%async_computation.2 | async-start | bytes 294912 | tf_op jit(solution)/shard_map/all_to_all | solution.py:210
  76.3 0.8 select_convert_fusion
  77.1 2.1 %collective-permute-start.4 = (bf16[512,512]{1,0:T(8,128)(2,1)S(1)}, bf16[512,512]{1,0:T(8,128)(2,1)}, u32[]{:S(2)}, u32[]{:S(2)}) collective-permute-start(bf16[512,512]{1,0:T(8,128)(2,1)S(1)} %collective-permute-done.3.refs_3_), channel_id=1, source_target_pairs={{0,1},{1,2},{2,3},{3,4},{4,5},{5,6},{6,7},{7,0},{8,9},{9,10},{10,1... | collective-permute-start | bytes 1572872 | tf_op jit(solution)/shard_map/ppermute | solution.py:206
  79.2 1.3 collective-permute-start.7
  80.5 5.9 %all-to-all-done.2 = f16[8,72,128]{2,1,0:T(8,128)(2,1)S(1)} async-done(((f16[8,72,128]{2,1,0:T(8,128)(2,1)}), f16[8,72,128]{2,1,0:T(8,128)(2,1)S(1)}, u32[]{:S(2)}, u32[]{:S(2)}) %all-to-all-start.2) | async-done | bytes 147488 | tf_op jit(solution)/shard_map/all_to_all | solution.py:210
  86.4 0.8 fusion.34
  87.2 1.7 %reshape.50 = f32[144,512]{1,0:T(8,128)} reshape(f32[8,72,128]{2,1,0:T(8,128)} %get-tuple-element.31) | data formatting | bytes 589824 | tf_op jit(solution)/shard_map/convert_element_type | solution.py:212
  88.9 1.0 convert_element_type.42
  89.9 1.0 subtract_convert_fusion
  90.9 0.0 collective-permute-done.12
  91.0 0.0 collective-permute-done.11
  91.0 6.8 %multiply_convert_fusion = f16[16,144,512]{2,1,0:T(8,128)(2,1)} fusion(bf16[16,144,288]{2,1,0:T(8,128)(2,1)S(1)} %select_convert_fusion, bf16[16,144,512]{2,1,0:T(8,128)(2,1)} %collective-permute-done.11, bf16[16,144,512]{2,1,0:T(8,128)(2,1)} %copy-done.4, bf16[144,512]{1,0:T(8,128)(2,1)S(1)} %subtract_convert_fusion, ...), kind=kOutput, calls=%fused_computation.15 | convolution fusion | flops 3121266688 | bytes 9748480 | tf_op jit(solution)/shard_map/kdt,tv->kdv/dot_general | solution.py:221
  97.8 0.0 collective-permute-done.4.refs_5_
  97.8 0.0 collective-permute-done.7.refs_6_
  97.8 7.2 %all-to-all-start.3 = ((f16[16,144,512]{2,1,0:T(8,128)(2,1)}), f16[16,144,512]{2,1,0:T(8,128)(2,1)}, u32[]{:S(2)}, u32[]{:S(2)}) async-start(f16[16,144,512]{2,1,0:T(8,128)(2,1)} %multiply_convert_fusion), calls=%async_computation.3 | async-start | bytes 4718592 | tf_op jit(solution)/shard_map/all_to_all | solution.py:223
  105.0 0.2 collective-permute-start.5
  105.3 0.1 stack.42.refs_0_
  105.3 2.5 %copy-done = bf16[256,16,576]{2,1,0:T(8,128)(2,1)S(1)} copy-done((bf16[256,16,576]{2,1,0:T(8,128)(2,1)S(1)}, bf16[256,16,576]{2,1,0:T(8,128)(2,1)}, u32[]{:S(2)}) %copy-start) | copy-done | bytes 4718616
  107.8 3.4 %shard_map.77.refs_5_ = f32[512,576]{1,0:T(8,128)S(1)} custom-call(s32[5]{0:T(128)S(1)} %stack.42.refs_0_, bf16[32,8,16,576]{3,2,1,0:T(8,128)(2,1)S(1)} %bitcast.23, bf16[512,512]{1,0:T(8,128)(2,1)S(1)} %multiply_convert_fusion.1.refs_2_, bf16[512,512]{1,0:T(8,128)(2,1)S(1)} %collective-permute-done.3.refs_3_, ...), custom_call_target="tpu_custom_call" | custom-call | flops 1509949440 | bytes 8388608 | tf_op jit(solution)/shard_map/pallas_call | solution.py:93
  111.3 3.1 %collective-permute-start.8 = (bf16[512,512]{1,0:T(8,128)(2,1)}, bf16[512,512]{1,0:T(8,128)(2,1)S(1)}, u32[]{:S(2)}, u32[]{:S(2)}) collective-permute-start(bf16[512,512]{1,0:T(8,128)(2,1)} %collective-permute-done.7.refs_6_), channel_id=1, source_target_pairs={{0,7},{1,0},{2,1},{3,2},{4,3},{5,4},{6,5},{7,6},{8,15},{9,8},{10,9... | collective-permute-start | bytes 1572872 | tf_op jit(solution)/shard_map/ppermute | solution.py:218
  114.4 0.6 log_subtract_fusion
  115.0 2.2 %collective-permute-done.5.refs_2_ = bf16[512,512]{1,0:T(8,128)(2,1)S(1)} collective-permute-done((bf16[512,512]{1,0:T(8,128)(2,1)}, bf16[512,512]{1,0:T(8,128)(2,1)S(1)}, u32[]{:S(2)}, u32[]{:S(2)}) %collective-permute-start.5) | collective-permute-done | bytes 524320 | tf_op jit(solution)/shard_map/ppermute | solution.py:217
  117.2 0.1 collective-permute-start.9
  117.3 15.7 %all-to-all-done.3 = f16[16,144,512]{2,1,0:T(8,128)(2,1)} async-done(((f16[16,144,512]{2,1,0:T(8,128)(2,1)}), f16[16,144,512]{2,1,0:T(8,128)(2,1)}, u32[]{:S(2)}, u32[]{:S(2)}) %all-to-all-start.3) | async-done | bytes 2359328 | tf_op jit(solution)/shard_map/all_to_all | solution.py:223
  133.0 2.0 %convert_reduce_fusion = f32[144,512]{1,0:T(8,128)S(1)} fusion(f16[16,144,512]{2,1,0:T(8,128)(2,1)} %all-to-all-done.3), kind=kLoop, calls=%fused_computation.14 | loop fusion | flops 2285568 | bytes 2654208 | tf_op jit(solution)/shard_map/reduce_sum | solution.py:232
  135.0 0.7 multiply_bitcast_fusion
  135.7 0.0 collective-permute-done.8.refs_3_
  135.7 0.1 collective-permute-start.10
  135.8 1.7 %constant_dynamic-slice_fusion.2 = (bf16[32,1,16,576]{3,2,1,0:T(8,128)(2,1)S(1)}, bf16[32,1,16,576]{3,2,1,0:T(8,128)(2,1)S(1)}, bf16[32,1,16,576]{3,2,1,0:T(8,128)(2,1)S(1)}) fusion(bf16[32,8,16,576]{3,2,1,0:T(8,128)(2,1)} %bitcast.22, s32[]{:T(128)S(6)} %select_n.96, s32[]{:T(128)S(6)} %select_n.100, s32[]{:T(128)S(6)} %select_n.98), kind=kLoop, calls=%fused_computation.54 | loop fusion | bytes 3538956 | tf_op jit(solution)/shard_map/jit(dynamic_index_in_dim)/dynamic_slice | solution.py:227
  137.5 0.3 pad_maximum_fusion.refs_1_
  137.8 0.0 collective-permute-done.9
  137.8 4.3 %collective-permute-done.10 = bf16[256,512]{1,0:T(8,128)(2,1)S(1)} collective-permute-done((bf16[256,512]{1,0:T(8,128)(2,1)S(1)}, bf16[256,512]{1,0:T(8,128)(2,1)S(1)}, u32[]{:S(2)}, u32[]{:S(2)}) %collective-permute-start.10) | collective-permute-done | bytes 262176 | tf_op jit(solution)/shard_map/ppermute | solution.py:226
  142.2 3.1 %shard_map.78 = f32[576,512]{1,0:T(8,128)} custom-call(s32[3]{0:T(128)S(1)} %stack.36.refs_0_, bf16[32,3,16,576]{3,2,1,0:T(8,128)(2,1)S(1)} %pad_maximum_fusion.refs_1_, bf16[512,512]{1,0:T(8,128)(2,1)S(1)} %collective-permute-done.5.refs_2_, bf16[512,512]{1,0:T(8,128)(2,1)S(1)} %collective-permute-done.8.refs_3_, ...), custom_call_target="tpu_custom_call" | custom-call | flops 905969664 | bytes 8388608 | tf_op jit(solution)/shard_map/pallas_call | solution.py:93
  (22 shorter events, 0.2 us)
Async XLA Ops:
  8.9 18.2 %all-to-all-start.1 = ((bf16[8,16,576]{2,1,0:T(8,128)(2,1)}), bf16[8,16,576]{2,1,0:T(8,128)(2,1)S(1)}, u32[]{:S(2)}, u32[]{:S(2)}) async-start(bf16[8,16,576]{2,1,0:T(8,128)(2,1)} %copy.10), calls=%async_computation.1 | async-start | bytes 327680 | tf_op jit(solution)/shard_map/all_to_all | solution.py:172
  17.4 87.9 %all-gather.3.cloned.1.call-start = ((), (), s32[]{:S(2)}) async-start(), calls=%async_computation.4 | async-start | bytes 5406720 | tf_op jit(solution)/shard_map/all_gather | solution.py:181
  18.1 9.7 %copy-start.2 = (bf16[512,576]{0,1:T(8,128)(2,1)S(1)}, bf16[512,576]{0,1:T(8,128)(2,1)}, u32[]{:S(2)}) copy-start(bf16[512,576]{0,1:T(8,128)(2,1)} %param.9) | copy-start | bytes 1769476
  18.1 9.7 %copy-start.3 = (s32[512]{0:T(512)S(1)}, s32[512]{0:T(512)}, u32[]{:S(2)}) copy-start(s32[512]{0:T(512)} %param.8) | copy-start | bytes 6148
  27.2 0.7 copy-start.5
  28.9 27.1 %all-to-all-start = ((bf16[32,80,128]{2,1,0:T(8,128)(2,1)}), bf16[32,80,128]{2,1,0:T(8,128)(2,1)S(1)}, u32[]{:S(2)}, u32[]{:S(2)}) async-start(bf16[32,80,128]{2,1,0:T(8,128)(2,1)} %shard_map.76), calls=%async_computation | async-start | bytes 1310720 | tf_op jit(solution)/shard_map/all_to_all | solution.py:185
  36.5 3.7 %collective-permute-start = (f32[2,512]{1,0:T(2,128)S(1)}, f32[2,512]{1,0:T(2,128)S(1)}, u32[]{:S(2)}, u32[]{:S(2)}) collective-permute-start(f32[2,512]{1,0:T(2,128)S(1)} %pad_maximum_fusion.2), channel_id=1, source_target_pairs={{0,1},{1,0},{2,3},{3,2},{4,5},{5,4},{6,7},{7,6},{8,9},{9,8},{10,11... | collective-permute-start | bytes 12296 | tf_op jit(solution)/shard_map/ppermute | solution.py:180
  40.2 4.6 %collective-permute-start.1 = (f32[2,512]{1,0:T(2,128)S(1)}, f32[2,512]{1,0:T(2,128)S(1)}, u32[]{:S(2)}, u32[]{:S(2)}) collective-permute-start(f32[2,512]{1,0:T(2,128)S(1)} %fusion.33), channel_id=1, source_target_pairs={{0,2},{1,3},{2,0},{3,1},{4,6},{5,7},{6,4},{7,5},{8,10},{9,11},{10,... | collective-permute-start | bytes 12296 | tf_op jit(solution)/shard_map/ppermute | solution.py:184
  44.9 11.1 %collective-permute-start.2 = (f32[2,512]{1,0:T(2,128)S(1)}, f32[2,512]{1,0:T(2,128)S(1)}, u32[]{:S(2)}, u32[]{:S(2)}) collective-permute-start(f32[2,512]{1,0:T(2,128)S(1)} %add.118), channel_id=1, source_target_pairs={{0,4},{1,5},{2,6},{3,7},{4,0},{5,1},{6,2},{7,3},{8,12},{9,13},{10,... | collective-permute-start | bytes 12296 | tf_op jit(solution)/shard_map/ppermute | solution.py:187
  49.2 2.4 %copy-start.1 = (bf16[512,4608]{1,0:T(8,128)(2,1)S(1)}, bf16[512,4608]{1,0:T(8,128)(2,1)}, u32[]{:S(2)}) copy-start(bf16[512,4608]{1,0:T(8,128)(2,1)} %x_ref) | copy-start | bytes 14155780
  54.6 1.4 copy-start.4
  56.0 35.0 %collective-permute-start.11 = (bf16[16,144,512]{2,1,0:T(8,128)(2,1)}, bf16[16,144,512]{2,1,0:T(8,128)(2,1)}, u32[]{:S(2)}, u32[]{:S(2)}) collective-permute-start(bf16[16,144,512]{2,1,0:T(8,128)(2,1)} %get-tuple-element.21), channel_id=1, source_target_pairs={{0,8},{8,0},{16,24},{24,16},{32,40},{40,32},{48,56},{56,48},{64,72... | collective-permute-start | bytes 7077896 | tf_op jit(solution)/shard_map/ppermute | solution.py:199
  56.5 15.6 %collective-permute-start.3 = (bf16[512,512]{1,0:T(8,128)(2,1)S(1)}, bf16[512,512]{1,0:T(8,128)(2,1)S(1)}, u32[]{:S(2)}, u32[]{:S(2)}) collective-permute-start(bf16[512,512]{1,0:T(8,128)(2,1)S(1)} %multiply_convert_fusion.1.refs_2_), channel_id=1, source_target_pairs={{0,1},{1,2},{2,3},{3,4},{4,5},{5,6},{6,7},{7,0},{8,9},{9,10},{10,1... | collective-permute-start | bytes 1572872 | tf_op jit(solution)/shard_map/ppermute | solution.py:195
  57.0 15.0 %collective-permute-start.6 = (bf16[512,512]{1,0:T(8,128)(2,1)S(1)}, bf16[512,512]{1,0:T(8,128)(2,1)S(1)}, u32[]{:S(2)}, u32[]{:S(2)}) collective-permute-start(bf16[512,512]{1,0:T(8,128)(2,1)S(1)} %multiply_convert_fusion.1.refs_2_), channel_id=1, source_target_pairs={{0,7},{1,0},{2,1},{3,2},{4,3},{5,4},{6,5},{7,6},{8,15},{9,8},{10,9... | collective-permute-start | bytes 1572872 | tf_op jit(solution)/shard_map/ppermute | solution.py:195
  59.8 31.2 %collective-permute-start.12 = (bf16[512,512]{1,0:T(8,128)(2,1)S(1)}, bf16[512,512]{1,0:T(8,128)(2,1)}, u32[]{:S(2)}, u32[]{:S(2)}) collective-permute-start(bf16[512,512]{1,0:T(8,128)(2,1)S(1)} %multiply_convert_fusion.1.refs_2_), channel_id=1, source_target_pairs={{0,8},{8,0},{16,24},{24,16},{32,40},{40,32},{48,56},{56,48},{64,72... | collective-permute-start | bytes 1572872 | tf_op jit(solution)/shard_map/ppermute | solution.py:196
  72.1 14.3 %all-to-all-start.2 = ((f16[8,72,128]{2,1,0:T(8,128)(2,1)}), f16[8,72,128]{2,1,0:T(8,128)(2,1)S(1)}, u32[]{:S(2)}, u32[]{:S(2)}) async-start(f16[8,72,128]{2,1,0:T(8,128)(2,1)} %reshape.49), calls=%async_computation.2 | async-start | bytes 294912 | tf_op jit(solution)/shard_map/all_to_all | solution.py:210
  77.1 20.7 %collective-permute-start.4 = (bf16[512,512]{1,0:T(8,128)(2,1)S(1)}, bf16[512,512]{1,0:T(8,128)(2,1)}, u32[]{:S(2)}, u32[]{:S(2)}) collective-permute-start(bf16[512,512]{1,0:T(8,128)(2,1)S(1)} %collective-permute-done.3.refs_3_), channel_id=1, source_target_pairs={{0,1},{1,2},{2,3},{3,4},{4,5},{5,6},{6,7},{7,0},{8,9},{9,10},{10,1... | collective-permute-start | bytes 1572872 | tf_op jit(solution)/shard_map/ppermute | solution.py:206
  79.2 18.6 %collective-permute-start.7 = (bf16[512,512]{1,0:T(8,128)(2,1)S(1)}, bf16[512,512]{1,0:T(8,128)(2,1)}, u32[]{:S(2)}, u32[]{:S(2)}) collective-permute-start(bf16[512,512]{1,0:T(8,128)(2,1)S(1)} %collective-permute-done.6.refs_4_), channel_id=1, source_target_pairs={{0,7},{1,0},{2,1},{3,2},{4,3},{5,4},{6,5},{7,6},{8,15},{9,8},{10,9... | collective-permute-start | bytes 1572872 | tf_op jit(solution)/shard_map/ppermute | solution.py:206
  97.8 35.2 %all-to-all-start.3 = ((f16[16,144,512]{2,1,0:T(8,128)(2,1)}), f16[16,144,512]{2,1,0:T(8,128)(2,1)}, u32[]{:S(2)}, u32[]{:S(2)}) async-start(f16[16,144,512]{2,1,0:T(8,128)(2,1)} %multiply_convert_fusion), calls=%async_computation.3 | async-start | bytes 4718592 | tf_op jit(solution)/shard_map/all_to_all | solution.py:223
  105.0 12.1 %collective-permute-start.5 = (bf16[512,512]{1,0:T(8,128)(2,1)}, bf16[512,512]{1,0:T(8,128)(2,1)S(1)}, u32[]{:S(2)}, u32[]{:S(2)}) collective-permute-start(bf16[512,512]{1,0:T(8,128)(2,1)} %collective-permute-done.4.refs_5_), channel_id=1, source_target_pairs={{0,1},{1,2},{2,3},{3,4},{4,5},{5,6},{6,7},{7,0},{8,9},{9,10},{10,1... | collective-permute-start | bytes 1572872 | tf_op jit(solution)/shard_map/ppermute | solution.py:217
  105.3 2.5 %copy-start = (bf16[256,16,576]{2,1,0:T(8,128)(2,1)S(1)}, bf16[256,16,576]{2,1,0:T(8,128)(2,1)}, u32[]{:S(2)}) copy-start(bf16[256,16,576]{2,1,0:T(8,128)(2,1)} %all-gather.3.cloned.1.call-done) | copy-start | bytes 14155780
  111.3 24.4 %collective-permute-start.8 = (bf16[512,512]{1,0:T(8,128)(2,1)}, bf16[512,512]{1,0:T(8,128)(2,1)S(1)}, u32[]{:S(2)}, u32[]{:S(2)}) collective-permute-start(bf16[512,512]{1,0:T(8,128)(2,1)} %collective-permute-done.7.refs_6_), channel_id=1, source_target_pairs={{0,7},{1,0},{2,1},{3,2},{4,3},{5,4},{6,5},{7,6},{8,15},{9,8},{10,9... | collective-permute-start | bytes 1572872 | tf_op jit(solution)/shard_map/ppermute | solution.py:218
  117.2 20.7 %collective-permute-start.9 = (bf16[256,512]{1,0:T(8,128)(2,1)S(1)}, bf16[256,512]{1,0:T(8,128)(2,1)S(1)}, u32[]{:S(2)}, u32[]{:S(2)}) collective-permute-start(bf16[256,512]{1,0:T(8,128)(2,1)S(1)} %slice.16), channel_id=1, source_target_pairs={{0,1},{1,2},{2,3},{3,4},{4,5},{5,6},{6,7},{7,0},{8,9},{9,10},{10,1... | collective-permute-start | bytes 786440 | tf_op jit(solution)/shard_map/ppermute | solution.py:226
  135.7 6.5 %collective-permute-start.10 = (bf16[256,512]{1,0:T(8,128)(2,1)S(1)}, bf16[256,512]{1,0:T(8,128)(2,1)S(1)}, u32[]{:S(2)}, u32[]{:S(2)}) collective-permute-start(bf16[256,512]{1,0:T(8,128)(2,1)S(1)} %slice.17), channel_id=1, source_target_pairs={{0,7},{1,0},{2,1},{3,2},{4,3},{5,4},{6,5},{7,6},{8,15},{9,8},{10,9... | collective-permute-start | bytes 786440 | tf_op jit(solution)/shard_map/ppermute | solution.py:226
Sparse Core Ops, SparseCore 0:
  28.0 53.6 all-gather.2
